TPU v7x, 128 devices: a whole 4x4x4 slice. The times are simulated.
128 devices in a mesh: dp: 64 (over x, z, y_lo, core), tensor: 2 (over y_hi).
Axes of the slice: x: 4, y: 4 (y_hi: 2, y_lo: 2; y = y_hi * 2 + y_lo), z: 4, core: 2. Of those that a mesh axis runs over, the one named last changes fastest.
Arguments:
- tokens: bfloat16 [32768, 1024], P(('dp', 'tensor')), may hold values from -6 to 6
- w_qkv: bfloat16 [1, 1024, 3, 1024], P(None, 'dp', None, 'tensor'), may hold values from -0.25 to 0.25
- b_qv: bfloat16 [1, 2, 1024], replicated, may hold values from -3 to 3
- w_out: bfloat16 [1, 1024, 1024], P(None, 'tensor', 'dp'), may hold values from -1 to 1
- b_out: bfloat16 [1, 1024], replicated, may hold values from -3 to 3
- gain_attn: bfloat16 [1, 1024], replicated, may hold values from 0.5 to 1.5
- shift_attn: bfloat16 [1, 1024], replicated, may hold values from -3 to 3
- w_in: bfloat16 [1, 1024, 4096], P(None, 'dp', 'tensor'), may hold values from -0.1875 to 0.1875
- b_in: bfloat16 [1, 4096], replicated, may hold values from -3 to 3
- w_back: bfloat16 [1, 4096, 1024], P(None, 'tensor', 'dp'), may hold values from -0.125 to 0.125
- b_back: bfloat16 [1, 1024], replicated, may hold values from -3 to 3
- gain_ffn: bfloat16 [1, 1024], replicated, may hold values from 0.5 to 1.5
- shift_ffn: bfloat16 [1, 1024], replicated, may hold values from -3 to 3
- cotangent: bfloat16 [32768, 1024], P(('dp', 'tensor')), may hold values from -6 to 6
Outputs:
- encoded: bfloat16 [32768, 1024], P(('dp', 'tensor'))
- grad_tokens: float32 [32768, 1024], P(('dp', 'tensor'))
- grad_w_qkv: float32 [1, 1024, 3, 1024], P(None, 'dp', None, 'tensor')
- grad_b_qv: float32 [1, 2, 1024], replicated
- grad_w_out: float32 [1, 1024, 1024], P(None, 'tensor', 'dp')
- grad_b_out: float32 [1, 1024], replicated
- grad_gain_attn: float32 [1, 1024], replicated
- grad_shift_attn: float32 [1, 1024], replicated
- grad_w_in: float32 [1, 1024, 4096], P(None, 'dp', 'tensor')
- grad_b_in: float32 [1, 4096], replicated
- grad_w_back: float32 [1, 4096, 1024], P(None, 'tensor', 'dp')
- grad_b_back: float32 [1, 1024], replicated
- grad_gain_ffn: float32 [1, 1024], replicated
- grad_shift_ffn: float32 [1, 1024], replicated
All inputs are finite; a program needn't handle non-finite values.
Results may differ from a plain program's by a relative error of at most 0.019.
Values may be sent and summed in bfloat16 or wider, within the bound.
A program may use at most 128 MiB of HBM per device.

v0:
```python
import jax
import jax.numpy as jnp
from jax import lax
from jax.sharding import PartitionSpec as P

HD = 64


epsilon = 1e-05
root_half = 0.7071067811865476
inv_root_tau = 0.3989422804014327


def gelu_exact(values):
    return 0.5 * values * (1.0 + lax.erf(values * root_half))


def gelu_slope(values):
    return (
        0.5 * (1.0 + lax.erf(values * root_half))
        + values * jnp.exp(-0.5 * values * values) * inv_root_tau
    )


def norm_forward(stream, gain, shift):
    center = stream - jnp.mean(stream, axis=-1, keepdims=True)
    inverse = lax.rsqrt(jnp.mean(center * center, axis=-1, keepdims=True) + epsilon)
    normed = center * inverse
    return (normed * gain + shift, normed, inverse)


def norm_backward(grad_out, normed, inverse, gain):
    scaled = grad_out * gain
    return inverse * (
        scaled
        - jnp.mean(scaled, axis=-1, keepdims=True)
        - normed * jnp.mean(scaled * normed, axis=-1, keepdims=True)
    )


def split_heads(matrix):
    return matrix.reshape(matrix.shape[0], matrix.shape[1] // HD, HD)


def attend_forward(query, keys, values):
    scores = jnp.einsum(
        "shd,thd->hst", split_heads(query), split_heads(keys), preferred_element_type=jnp.float32
    ) * HD ** (-0.5)
    highest = jnp.max(scores, axis=-1, keepdims=True)
    weights = jnp.exp(scores - highest)
    totals = jnp.sum(weights, axis=-1, keepdims=True)
    probs_low = (weights / totals).astype(jnp.bfloat16)
    mixed = jnp.einsum(
        "hst,thd->shd", probs_low, split_heads(values), preferred_element_type=jnp.float32
    )
    return (mixed.reshape(query.shape), highest + jnp.log(totals))


def attend_backward(query, keys, values, log_total, grad_mixed):
    scale = HD ** (-0.5)
    query_heads = split_heads(query)
    key_heads = split_heads(keys)
    value_heads = split_heads(values)
    grad_heads = split_heads(grad_mixed)
    scores = (
        jnp.einsum("shd,thd->hst", query_heads, key_heads, preferred_element_type=jnp.float32)
        * scale
    )
    probs_full = jnp.exp(scores - log_total)
    grad_probs = jnp.einsum(
        "shd,thd->hst", grad_heads, value_heads, preferred_element_type=jnp.float32
    )
    row_dot = jnp.sum(probs_full * grad_probs, axis=-1, keepdims=True)
    grad_scores = (probs_full * (grad_probs - row_dot)).astype(jnp.bfloat16)
    grad_values = jnp.einsum(
        "hst,shd->thd",
        probs_full.astype(jnp.bfloat16),
        grad_heads,
        preferred_element_type=jnp.float32,
    )
    grad_query = (
        jnp.einsum("hst,thd->shd", grad_scores, key_heads, preferred_element_type=jnp.float32)
        * scale
    )
    grad_keys = (
        jnp.einsum("hst,shd->thd", grad_scores, query_heads, preferred_element_type=jnp.float32)
        * scale
    )
    full_shape = query.shape
    return (
        grad_query.reshape(full_shape).astype(jnp.bfloat16),
        grad_keys.reshape(full_shape).astype(jnp.bfloat16),
        grad_values.reshape(full_shape).astype(jnp.bfloat16),
    )


def local_slice(vector, width, dim):
    return lax.dynamic_slice_in_dim(vector, lax.axis_index("tensor") * width, width, dim)


def widen(piece, full_width, dim):
    target = list(piece.shape)
    target[dim] = full_width
    return lax.dynamic_update_slice_in_dim(
        jnp.zeros(target, jnp.float32), piece, lax.axis_index("tensor") * piece.shape[dim], dim
    )


def fetch_forward(shards):
    return (
        lax.all_gather(shards[0], "dp", axis=0, tiled=True),
        lax.all_gather(shards[1], "dp", axis=1, tiled=True),
        lax.all_gather(shards[2], "dp", axis=0, tiled=True),
        lax.all_gather(shards[3], "dp", axis=1, tiled=True),
    )


def fetch_backward(shards):
    return (
        lax.all_gather(shards[0], "dp", axis=0, tiled=True),
        lax.all_gather(shards[1], "dp", axis=1, tiled=True),
        lax.all_gather(shards[2], "dp", axis=0, tiled=True),
        lax.all_gather(shards[3], "dp", axis=1, tiled=True),
    )


def body(
    tokens,
    w_qkv,
    b_qv,
    w_out,
    b_out,
    gain_attn,
    shift_attn,
    w_in,
    b_in,
    w_back,
    b_back,
    gain_ffn,
    shift_ffn,
    cotangent,
):
    layers = w_qkv.shape[0]
    head_width = w_qkv.shape[3]
    hidden_width = w_in.shape[2]
    model_width = tokens.shape[1]
    ff_width = b_in.shape[1]
    stream = tokens.astype(jnp.float32)
    layer_index = 0
    shards = (w_qkv[layer_index], w_out[layer_index], w_in[layer_index], w_back[layer_index])
    full_qkv, full_out, full_in, full_back = fetch_forward(shards)
    seq_rows = lax.all_gather(stream.astype(jnp.bfloat16), "tensor", axis=0, tiled=True)
    projected = jnp.einsum("sd,dcf->scf", seq_rows, full_qkv, preferred_element_type=jnp.float32)
    bias_here = local_slice(b_qv[layer_index].astype(jnp.float32), head_width, 1)
    query = (projected[:, 0] + bias_here[0]).astype(jnp.bfloat16)
    keys = projected[:, 1].astype(jnp.bfloat16)
    values = (projected[:, 2] + bias_here[1]).astype(jnp.bfloat16)
    mixed, log_total = attend_forward(query, keys, values)
    mixed_low = mixed.astype(jnp.bfloat16)
    attn_part = jnp.dot(mixed_low, full_out, preferred_element_type=jnp.float32)
    attended = lax.psum_scatter(
        attn_part.astype(jnp.bfloat16), "tensor", scatter_dimension=0, tiled=True
    ).astype(jnp.float32)
    hidden, normed1, inverse1 = norm_forward(
        stream + attended + b_out[layer_index].astype(jnp.float32),
        gain_attn[layer_index].astype(jnp.float32),
        shift_attn[layer_index].astype(jnp.float32),
    )
    hidden_rows = lax.all_gather(hidden.astype(jnp.bfloat16), "tensor", axis=0, tiled=True)
    upward = jnp.dot(hidden_rows, full_in, preferred_element_type=jnp.float32) + local_slice(
        b_in[layer_index].astype(jnp.float32), hidden_width, 0
    )
    activated = gelu_exact(upward).astype(jnp.bfloat16)
    down_part = jnp.dot(activated, full_back, preferred_element_type=jnp.float32)
    downward = lax.psum_scatter(
        down_part.astype(jnp.bfloat16), "tensor", scatter_dimension=0, tiled=True
    ).astype(jnp.float32)
    stream, normed2, inverse2 = norm_forward(
        hidden + downward + b_back[layer_index].astype(jnp.float32),
        gain_ffn[layer_index].astype(jnp.float32),
        shift_ffn[layer_index].astype(jnp.float32),
    )
    saved = [
        (
            seq_rows,
            query,
            keys,
            values,
            log_total,
            mixed_low,
            normed1,
            inverse1,
            hidden_rows,
            upward,
            activated,
            normed2,
            inverse2,
        )
    ]
    encoded = stream.astype(jnp.bfloat16)
    grad = cotangent.astype(jnp.float32)
    weight_parts = [None] * layers
    small_parts = [None] * layers
    for layer_index in reversed(range(layers)):
        (
            seq_rows,
            query,
            keys,
            values,
            log_total,
            mixed_low,
            normed1,
            inverse1,
            hidden_rows,
            upward,
            activated,
            normed2,
            inverse2,
        ) = saved[layer_index]
        shards = (w_qkv[layer_index], w_out[layer_index], w_in[layer_index], w_back[layer_index])
        full_qkv, full_out, full_in, full_back = fetch_backward(shards)
        d_gain2 = jnp.sum(grad * normed2, axis=0)
        d_shift2 = jnp.sum(grad, axis=0)
        grad_r2 = norm_backward(grad, normed2, inverse2, gain_ffn[layer_index].astype(jnp.float32))
        d_bias_back = jnp.sum(grad_r2, axis=0)
        grad_down = lax.all_gather(grad_r2.astype(jnp.bfloat16), "tensor", axis=0, tiled=True)
        g_back = jnp.einsum("sf,sd->fd", activated, grad_down, preferred_element_type=jnp.float32)
        grad_act = jnp.einsum("sd,fd->sf", grad_down, full_back, preferred_element_type=jnp.float32)
        grad_up = (grad_act * gelu_slope(upward)).astype(jnp.bfloat16)
        d_bias_in = jnp.sum(grad_up.astype(jnp.float32), axis=0)
        g_in = jnp.einsum("sd,sf->df", hidden_rows, grad_up, preferred_element_type=jnp.float32)
        grad_hidden_part = jnp.einsum(
            "sf,df->sd", grad_up, full_in, preferred_element_type=jnp.float32
        )
        grad_hidden = grad_r2 + lax.psum_scatter(
            grad_hidden_part.astype(jnp.bfloat16), "tensor", scatter_dimension=0, tiled=True
        ).astype(jnp.float32)
        d_gain1 = jnp.sum(grad_hidden * normed1, axis=0)
        d_shift1 = jnp.sum(grad_hidden, axis=0)
        grad_r1 = norm_backward(
            grad_hidden, normed1, inverse1, gain_attn[layer_index].astype(jnp.float32)
        )
        d_bias_out = jnp.sum(grad_r1, axis=0)
        grad_att = lax.all_gather(grad_r1.astype(jnp.bfloat16), "tensor", axis=0, tiled=True)
        g_out = jnp.einsum("sh,sd->hd", mixed_low, grad_att, preferred_element_type=jnp.float32)
        grad_mixed = jnp.einsum(
            "sd,hd->sh", grad_att, full_out, preferred_element_type=jnp.float32
        ).astype(jnp.bfloat16)
        grad_query, grad_keys, grad_values = attend_backward(
            query, keys, values, log_total, grad_mixed
        )
        grad_proj = jnp.stack([grad_query, grad_keys, grad_values], axis=1)
        g_qkv = jnp.einsum("sd,scf->dcf", seq_rows, grad_proj, preferred_element_type=jnp.float32)
        d_bias_qv = jnp.stack(
            [
                jnp.sum(grad_query.astype(jnp.float32), axis=0),
                jnp.sum(grad_values.astype(jnp.float32), axis=0),
            ]
        )
        grad_rows_part = jnp.einsum(
            "scf,dcf->sd", grad_proj, full_qkv, preferred_element_type=jnp.float32
        )
        grad = grad_r1 + lax.psum_scatter(
            grad_rows_part.astype(jnp.bfloat16), "tensor", scatter_dimension=0, tiled=True
        ).astype(jnp.float32)
        weight_parts[layer_index] = (
            lax.psum_scatter(g_qkv, "dp", scatter_dimension=0, tiled=True),
            lax.psum_scatter(g_out, "dp", scatter_dimension=1, tiled=True),
            lax.psum_scatter(g_in, "dp", scatter_dimension=0, tiled=True),
            lax.psum_scatter(g_back, "dp", scatter_dimension=1, tiled=True),
        )
        small_parts[layer_index] = lax.psum(
            (
                widen(d_bias_qv, model_width, 1),
                d_bias_out,
                d_gain1,
                d_shift1,
                widen(d_bias_in, ff_width, 0),
                d_bias_back,
                d_gain2,
                d_shift2,
            ),
            ("dp", "tensor"),
        )

    def stack_weights(slot):
        return jnp.stack([weight_parts[0][slot]])

    def stack_small(slot):
        return jnp.stack([small_parts[0][slot]])

    return (
        encoded,
        grad,
        stack_weights(0),
        stack_small(0),
        stack_weights(1),
        stack_small(1),
        stack_small(2),
        stack_small(3),
        stack_weights(2),
        stack_small(4),
        stack_weights(3),
        stack_small(5),
        stack_small(6),
        stack_small(7),
    )


def solution(mesh):
    in_specs = (
        P(("dp", "tensor"), None),
        P(None, "dp", None, "tensor"),
        P(),
        P(None, "tensor", "dp"),
        P(),
        P(),
        P(),
        P(None, "dp", "tensor"),
        P(),
        P(None, "tensor", "dp"),
        P(),
        P(),
        P(),
        P(("dp", "tensor"), None),
    )
    out_specs = (
        P(("dp", "tensor"), None),
        P(("dp", "tensor"), None),
        P(None, "dp", None, "tensor"),
        P(),
        P(None, "tensor", "dp"),
        P(),
        P(),
        P(),
        P(None, "dp", "tensor"),
        P(),
        P(None, "tensor", "dp"),
        P(),
        P(),
        P(),
    )
    return jax.shard_map(body, mesh=mesh, in_specs=in_specs, out_specs=out_specs, check_vma=False)
```

profile of v0, /device:TPU:1, one launch (start us, length us, event | category | flops | bytes accessed | tf_op | source)
XLA Modules:
  0.0 2150.2 jit_solution(10079528183127447212)
XLA Ops:
  10.3 28.0 %all-gather.13.cloned.1.call-done = bf16[512,1024]{1,0:T(8,128)(2,1)} async-done(((bf16[256,1024]{1,0:T(8,128)(2,1)}), bf16[512,1024]{1,0:T(8,128)(2,1)}) %all-gather.13.cloned.1.call-update) | async-done | bytes 1048592 | tf_op jit(solution)/shard_map/all_gather | solution.py:152
  38.3 106.4 %all-gather.21.cloned.1.call-done = bf16[1,1024,3,512]{3,1,2,0:T(8,128)(2,1)} async-done(((bf16[1,16,3,512]{3,1,2,0:T(8,128)(2,1)}), bf16[1,1024,3,512]{3,1,2,0:T(8,128)(2,1)}) %all-gather.21.cloned.1.call-update) | async-done | bytes 3145744 | tf_op jit(solution)/shard_map/all_gather | solution.py:111
  144.6 4.1 fusion.23
  155.7 91.2 %all-gather.23.cloned.1.call-done = bf16[1,512,1024]{1,2,0:T(8,128)(2,1)} async-done(((bf16[1,512,16]{1,2,0:T(8,128)(2,1)}), bf16[1,512,1024]{1,2,0:T(8,128)(2,1)}) %all-gather.23.cloned.1.call-update) | async-done | bytes 1048592 | tf_op jit(solution)/shard_map/all_gather | solution.py:112
  246.9 3.0 convolution_convert_fusion
  250.6 22.4 %reduce-scatter.8.cloned.1.call-done = bf16[256,1024]{1,0:T(8,128)(2,1)} async-done(((bf16[512,1024]{1,0:T(8,128)(2,1)}), bf16[256,1024]{1,0:T(8,128)(2,1)}) %reduce-scatter.8.cloned.1.call-update) | async-done | bytes 524304 | tf_op jit(solution)/shard_map/reduce_scatter | solution.py:161
  278.8 101.6 %all-gather.25.cloned.1.call-done = bf16[1,1024,2048]{2,1,0:T(8,128)(2,1)} async-done(((bf16[1,16,2048]{2,1,0:T(8,128)(2,1)}), bf16[1,1024,2048]{2,1,0:T(8,128)(2,1)}) %all-gather.25.cloned.1.call-update) | async-done | bytes 4194320 | tf_op jit(solution)/shard_map/all_gather | solution.py:113
  380.4 26.2 %all-gather.15.cloned.1.call-done = bf16[512,1024]{1,0:T(8,128)(2,1)} async-done(((bf16[256,1024]{1,0:T(8,128)(2,1)}), bf16[512,1024]{1,0:T(8,128)(2,1)}) %all-gather.15.cloned.1.call-update) | async-done | bytes 1048592 | tf_op jit(solution)/shard_map/all_gather | solution.py:169
  406.6 7.7 multiply_convert_fusion.1
  414.4 99.9 %all-gather.27.cloned.1.call-done = bf16[1,2048,1024]{1,2,0:T(8,128)(2,1)} async-done(((bf16[1,2048,16]{1,2,0:T(8,128)(2,1)}), bf16[1,2048,1024]{1,2,0:T(8,128)(2,1)}) %all-gather.27.cloned.1.call-update) | async-done | bytes 4194320 | tf_op jit(solution)/shard_map/all_gather | solution.py:114
  514.2 6.2 fusion.32
  520.6 23.0 %reduce-scatter.10.cloned.1.call-done = bf16[256,1024]{1,0:T(8,128)(2,1)} async-done(((bf16[512,1024]{1,0:T(8,128)(2,1)}), bf16[256,1024]{1,0:T(8,128)(2,1)}) %reduce-scatter.10.cloned.1.call-update) | async-done | bytes 524304 | tf_op jit(solution)/shard_map/reduce_scatter | solution.py:175
  547.1 2.8 fusion.63
  550.0 24.9 %all-gather.17.cloned.1.call-done = bf16[512,1024]{1,0:T(8,128)(2,1)} async-done(((bf16[256,1024]{1,0:T(8,128)(2,1)}), bf16[512,1024]{1,0:T(8,128)(2,1)}) %all-gather.17.cloned.1.call-update) | async-done | bytes 1048592 | tf_op jit(solution)/shard_map/all_gather | solution.py:226
  574.8 6.4 convert_reduce_fusion
  582.6 3.3 fusion.29
  586.1 23.9 %reduce-scatter.12.cloned.1.call-done = bf16[256,1024]{1,0:T(8,128)(2,1)} async-done(((bf16[512,1024]{1,0:T(8,128)(2,1)}), bf16[256,1024]{1,0:T(8,128)(2,1)}) %reduce-scatter.12.cloned.1.call-update) | async-done | bytes 524304 | tf_op jit(solution)/shard_map/reduce_scatter | solution.py:235
  614.8 24.6 %all-gather.19.cloned.1.call-done = bf16[512,1024]{1,0:T(8,128)(2,1)} async-done(((bf16[256,1024]{1,0:T(8,128)(2,1)}), bf16[512,1024]{1,0:T(8,128)(2,1)}) %all-gather.19.cloned.1.call-update) | async-done | bytes 1048592 | tf_op jit(solution)/shard_map/all_gather | solution.py:244
  639.4 2.3 convolution_convert_fusion.1
  641.7 5.2 convert_reduce_fusion.2
  646.9 4.8 multiply_reduce_fusion
  651.8 2.6 multiply_convert_fusion
  658.2 4.7 bitcast_convert_fusion
  663.0 5.8 convolution_bitcast_fusion
  668.7 9.4 copy.49
  682.0 7.5 fusion.68
  690.7 7.2 fusion.69
  700.0 66.2 %all-reduce.1 = (f32[1,2,1024]{2,1,0:T(2,128)}, f32[1,1024]{1,0:T(1,128)}, f32[1,1024]{1,0:T(1,128)}, f32[1,1024]{1,0:T(1,128)}, f32[1,4096]{1,0:T(1,128)}, /*in...) all-reduce(f32[1,2,1024]{2,1,0:T(2,128)S(1)} %fusion.56, ...), channel_id=1, replica_groups=mesh['dp'=64,'tensor'=2] {'dp','tensor'}, use_global_device_ids=true, to_apply=%region_18.0 | all-reduce | flops 12288 | bytes 98304 | tf_op jit(solution)/shard_map/psum | solution.py:272
  768.3 493.5 %all-reduce.4.cloned.1.call-done = f32[1024,3,512]{2,1,0:T(4,128)} async-done(((f32[1024,3,512]{2,1,0:T(4,128)}), f32[1024,3,512]{2,1,0:T(4,128)}) %all-reduce.4.cloned.1.call-update) | async-done | bytes 6291472
  1263.5 283.0 %reduce-scatter.16.cloned.1.call-done = f32[512,16]{0,1:T(8,128)} async-done(((f32[512,1024]{0,1:T(8,128)}), f32[512,16]{0,1:T(8,128)}) %reduce-scatter.16.cloned.1.call-update) | async-done | bytes 32784 | tf_op jit(solution)/shard_map/reduce_scatter | solution.py:268
  1546.5 298.5 %reduce-scatter.18.cloned.1.call-done = f32[16,2048]{1,0:T(8,128)} async-done(((f32[1024,2048]{1,0:T(8,128)}), f32[16,2048]{1,0:T(8,128)}) %reduce-scatter.18.cloned.1.call-update) | async-done | bytes 131088 | tf_op jit(solution)/shard_map/reduce_scatter | solution.py:269
  1845.0 298.3 %reduce-scatter.20.cloned.1.call-done = f32[2048,16]{0,1:T(8,128)} async-done(((f32[2048,1024]{0,1:T(8,128)}), f32[2048,16]{0,1:T(8,128)}) %reduce-scatter.20.cloned.1.call-update) | async-done | bytes 131088 | tf_op jit(solution)/shard_map/reduce_scatter | solution.py:270
  (133 shorter events, 40.2 us)
Async XLA Ops:
  7.2 31.1 %all-gather.13.cloned.1.call-start = ((), (), s32[]{:S(2)}) async-start(), calls=%async_computation.7 | async-start | bytes 1572864 | tf_op jit(solution)/shard_map/all_gather | solution.py:152
  7.9 136.7 %all-gather.21.cloned.1.call-start = ((), (), s32[]{:S(2)}) async-start(), calls=%async_computation.18 | async-start | bytes 3194880 | tf_op jit(solution)/shard_map/all_gather | solution.py:111
  8.7 238.2 %all-gather.23.cloned.1.call-start = ((), (), s32[]{:S(2)}) async-start(), calls=%async_computation.19 | async-start | bytes 1064960 | tf_op jit(solution)/shard_map/all_gather | solution.py:112
  9.4 263.6 %reduce-scatter.8.cloned.1.call-start = ((), (), s32[]{:S(2)}) async-start(), calls=%async_computation.8 | async-start | bytes 1572864 | tf_op jit(solution)/shard_map/reduce_scatter | solution.py:161
  150.4 3.2 copy-start
  153.6 96.9 %copy-start.13 = (bf16[1,1024]{1,0:T(2,128)(2,1)S(1)}, bf16[1,1024]{1,0:T(2,128)(2,1)}, u32[]{:S(2)}) copy-start(bf16[1,1024]{1,0:T(2,128)(2,1)} %param.20) | copy-start | bytes 6148
  153.6 97.0 %copy-start.14 = (bf16[1,1024]{1,0:T(2,128)(2,1)S(1)}, bf16[1,1024]{1,0:T(2,128)(2,1)}, u32[]{:S(2)}) copy-start(bf16[1,1024]{1,0:T(2,128)(2,1)} %param.19) | copy-start | bytes 6148
  153.6 97.0 %copy-start.15 = (bf16[1,1024]{1,0:T(2,128)(2,1)S(1)}, bf16[1,1024]{1,0:T(2,128)(2,1)}, u32[]{:S(2)}) copy-start(bf16[1,1024]{1,0:T(2,128)(2,1)} %param.18) | copy-start | bytes 6148
  155.6 122.9 %copy-start.10 = (bf16[8,64,512]{2,1,0:T(8,128)(2,1)}, bf16[8,64,512]{2,1,0:T(8,128)(2,1)S(1)}, u32[]{:S(2)}) copy-start(bf16[8,64,512]{2,1,0:T(8,128)(2,1)S(1)} %fusion.38) | copy-start | bytes 1572868
  155.6 117.3 %copy-start.1 = (bf16[256,1024]{1,0:T(8,128)(2,1)S(1)}, bf16[256,1024]{1,0:T(8,128)(2,1)}, u32[]{:S(2)}) copy-start(bf16[256,1024]{1,0:T(8,128)(2,1)} %param.14) | copy-start | bytes 1572868
  246.9 31.9 %copy-start.12 = (bf16[1,4096]{1,0:T(2,128)(2,1)S(1)}, bf16[1,4096]{1,0:T(2,128)(2,1)}, u32[]{:S(2)}) copy-start(bf16[1,4096]{1,0:T(2,128)(2,1)} %param.22) | copy-start | bytes 24580
  249.9 130.5 %all-gather.25.cloned.1.call-start = ((), (), s32[]{:S(2)}) async-start(), calls=%async_computation.20 | async-start | bytes 4259840 | tf_op jit(solution)/shard_map/all_gather | solution.py:113
  250.5 156.1 %all-gather.15.cloned.1.call-start = ((), (), s32[]{:S(2)}) async-start(), calls=%async_computation.9 | async-start | bytes 1572864 | tf_op jit(solution)/shard_map/all_gather | solution.py:169
  277.8 236.4 %all-gather.27.cloned.1.call-start = ((), (), s32[]{:S(2)}) async-start(), calls=%async_computation.21 | async-start | bytes 4259840 | tf_op jit(solution)/shard_map/all_gather | solution.py:114
  278.6 265.0 %reduce-scatter.10.cloned.1.call-start = ((), (), s32[]{:S(2)}) async-start(), calls=%async_computation.10 | async-start | bytes 1572864 | tf_op jit(solution)/shard_map/reduce_scatter | solution.py:175
  514.2 6.3 copy-start.16
  514.2 6.3 copy-start.17
  514.2 6.3 copy-start.18
  514.2 29.4 %copy-start.2 = (bf16[256,1024]{1,0:T(8,128)(2,1)S(1)}, bf16[256,1024]{1,0:T(8,128)(2,1)}, u32[]{:S(2)}) copy-start(bf16[256,1024]{1,0:T(8,128)(2,1)} %reduce-scatter.8.cloned.1.call-done) | copy-start | bytes 1572868
  520.5 54.4 %all-gather.17.cloned.1.call-start = ((), (), s32[]{:S(2)}) async-start(), calls=%async_computation.11 | async-start | bytes 1572864 | tf_op jit(solution)/shard_map/all_gather | solution.py:226
  549.9 60.0 %reduce-scatter.12.cloned.1.call-start = ((), (), s32[]{:S(2)}) async-start(), calls=%async_computation.12 | async-start | bytes 1572864 | tf_op jit(solution)/shard_map/reduce_scatter | solution.py:235
  574.8 7.8 copy-start.19
  582.6 27.3 %copy-start.3 = (f32[256,1024]{1,0:T(8,128)S(1)}, f32[256,1024]{1,0:T(8,128)}, u32[]{:S(2)}) copy-start(f32[256,1024]{1,0:T(8,128)} %get-tuple-element.64) | copy-start | bytes 3145732
  586.0 53.4 %all-gather.19.cloned.1.call-start = ((), (), s32[]{:S(2)}) async-start(), calls=%async_computation.13 | async-start | bytes 1572864 | tf_op jit(solution)/shard_map/all_gather | solution.py:244
  614.5 151.7 %reduce-scatter.14.cloned.1.call-start = ((), (), s32[]{:S(2)}) async-start(), calls=%async_computation.14 | async-start | bytes 1572864 | tf_op jit(solution)/shard_map/reduce_scatter | solution.py:263
  641.7 5.2 copy-start.7
  641.7 10.1 slice-start
  646.9 4.9 slice-start.1
  662.9 599.0 %all-reduce.4.cloned.1.call-start = ((), (), s32[]{:S(2)}) async-start(), calls=%async_computation.22 | async-start | bytes 16777216
  678.2 868.3 %reduce-scatter.16.cloned.1.call-start = ((), (), s32[]{:S(2)}) async-start(), calls=%async_computation.15 | async-start | bytes 2129920 | tf_op jit(solution)/shard_map/reduce_scatter | solution.py:268
  681.7 1163.3 %reduce-scatter.18.cloned.1.call-start = ((), (), s32[]{:S(2)}) async-start(), calls=%async_computation.16 | async-start | bytes 8519680 | tf_op jit(solution)/shard_map/reduce_scatter | solution.py:269
  689.5 1453.7 %reduce-scatter.20.cloned.1.call-start = ((), (), s32[]{:S(2)}) async-start(), calls=%async_computation.17 | async-start | bytes 8519680 | tf_op jit(solution)/shard_map/reduce_scatter | solution.py:270
  (9 other events, 13.5 us)
Sparse Core Ops, SparseCore 0:
  9.7 28.5 all-gather.12
  40.0 104.5 all-gather.20
  146.4 100.4 all-gather.22
  250.0 22.9 reduce-scatter.7
  274.6 105.7 all-gather.24
  382.6 23.9 all-gather.14
  408.5 105.7 all-gather.26
  520.6 22.9 reduce-scatter.9
  550.1 24.7 all-gather.16
  586.1 23.7 reduce-scatter.11
  614.6 24.7 all-gather.18
  663.0 23.7 reduce-scatter.13
  689.3 572.5 all-reduce.3
  1264.7 281.8 reduce-scatter.15
  1549.4 295.5 reduce-scatter.17
  1847.9 295.2 reduce-scatter.19
where the time goes:
time: 2160 us; the launch traced here: 2150 us
  waiting for transfers between devices  1950 us (90%)
  matrix products  76.8 us (4%)
  blocking collectives  66.2 us (3%)
  other arithmetic  22.5 us (1%)
    unnamed x17, waiting for transfers between devices  497 us
    reduce_scatter x1, waiting for transfers between devices, body(): lax.psum_scatter(g_in, 'dp', scatter_dimension=0, tiled=True)  298 us
    reduce_scatter x1, waiting for transfers between devices, body(): lax.psum_scatter(g_back, 'dp', scatter_dimension=1, tiled=True)  298 us
    reduce_scatter x1, waiting for transfers between devices, body(): lax.psum_scatter(g_out, 'dp', scatter_dimension=1, tiled=True)  283 us
    all_gather x1, waiting for transfers between devices, fetch_forward(): lax.all_gather(shards[0], 'dp', axis=0, tiled=True)  106 us
    all_gather x1, waiting for transfers between devices, fetch_forward(): lax.all_gather(shards[2], 'dp', axis=0, tiled=True)  102 us
    all_gather x1, waiting for transfers between devices, fetch_forward(): lax.all_gather(shards[3], 'dp', axis=1, tiled=True)  99.9 us
    all_gather x1, waiting for transfers between devices, fetch_forward(): lax.all_gather(shards[1], 'dp', axis=1, tiled=True)  91.2 us
  transfers between devices with their start and end apart: 16, of which 15 were waited for; matrix products, arithmetic and copies ran while one was open for 3% of the time, Pallas kernels for 0%

commit v1 on v0

v1 whole, which is shorter than its diff:
```python
import jax
import jax.numpy as jnp
from jax import lax
from jax.experimental import pallas as pl
from jax.experimental.pallas import tpu as pltpu
from jax.sharding import PartitionSpec as P

F32 = jnp.float32
BF16 = jnp.bfloat16
MESH = pl.DeviceIdType.MESH
EPS = 1e-05
ROOT_HALF = 0.7071067811865476
INV_ROOT_TAU = 0.3989422804014327

WIDTH = (768, 256, 1024, 1024)
BASE = (0, 768, 1024, 2048)
PIECES = (
    ((0, 0, 256), (1, 256, 256), (2, 512, 256)),
    ((0, 0, 128), (2, 128, 128)),
    ((0, 0, 384), (1, 384, 384), (2, 768, 256)),
    ((0, 0, 256), (1, 256, 384), (2, 640, 384)),
)
ORDER = (("x", "z", "y"), ("z", "y", "x"), ("y", "x", "z"))
PIECE_LIST = [(g, i) for g in range(4) for i in range(len(PIECES[g]))]
SLOT = {(g, i): n for n, (g, i) in enumerate(PIECE_LIST)}
NP = len(PIECE_LIST)


def block_dims(axes_all):
    return (
        2 if "y" in axes_all else 1,
        4 if "x" in axes_all else 1,
        4 if "z" in axes_all else 1,
        2 if "y" in axes_all else 1,
    )


def dot(a, b, ca, cb):
    return lax.dot_general(a, b, (((ca,), (cb,)), ((), ())), preferred_element_type=F32)


def kernel(*refs):
    refs = list(refs)

    def take(n):
        out = refs[:n]
        del refs[:n]
        return out

    pw, tok, cot, vec = take(4)
    enc_out, gtok_out, gw_out, small_out = take(4)
    W = take(4)
    G = [None] * 4
    (G[3],) = take(1)
    G[2], G[1], G[0] = W[3], W[1], W[2]
    (X, C, Q, K, V, PR, MX, N1, INV1, H, ACT, SL, GR, GD, GM, ENC, GTR) = take(17)
    DQ, DK, DV, GTS = Q, K, V, H.at[pl.ds(0, 256)]
    S, R1, R2, R3, R4 = take(5)
    ACC, SVA, SVB, EXA, EXB, FIN = take(6)
    rs1 = take(NP * 3)
    rs2 = take(NP * 3)
    (ag_send, ag_recv, rs_send, rs_recv, ex_send, ex_recv, io_send, io_recv, io_loc) = take(9)
    (sm_send, sm_recv, smx_send, smx_recv, pw_send, pw_recv, fin_send, fin_recv) = take(8)

    dp = lax.axis_index("dp")
    th = lax.axis_index("tensor")
    c = dp % 2
    yl = (dp // 2) % 2
    z = (dp // 4) % 4
    x = dp // 16
    y = th * 2 + yl
    me = {"x": x, "y": y, "z": z}

    def device(xx, yy, zz, cc):
        return (((xx * 4 + zz) * 2 + yy % 2) * 2 + cc, yy // 2)

    def nbr(axis, d):
        xx, yy, zz = x, y, z
        if axis == "x":
            xx = (x + d) % 4
        if axis == "y":
            yy = (y + d) % 4
        if axis == "z":
            zz = (z + d) % 4
        return device(xx, yy, zz, c)

    mate = device(x, y, z, 1 - c)
    partner = (((x * 4 + z) * 2 + yl) * 2 + (1 - c), 1 - th)
    stays = c == th

    def remote(src, dst, ss, rs, to):
        return pltpu.make_async_remote_copy(
            src_ref=src, dst_ref=dst, send_sem=ss, recv_sem=rs, device_id=to, device_id_type=MESH
        )

    barrier = pltpu.get_barrier_semaphore()
    talk = [nbr(a, d) for a in ("x", "y", "z") for d in (1, 2, 3)] + [mate, partner]
    for to in talk:
        pl.semaphore_signal(barrier, inc=1, device_id=to, device_id_type=MESH)
    pl.semaphore_wait(barrier, len(talk))

    def chip_rows(core):
        return pl.ds(pl.multiple_of(core * 16, 16), 16)

    def own_slot(ref, rows, cols):
        return ref.at[th, x, z, yl, rows, cols]

    def pw_copy(g):
        cols = pl.ds(BASE[g], WIDTH[g])
        return remote(
            pw.at[1 - c, :, cols],
            own_slot(W[g], chip_rows(c), pl.ds(0, WIDTH[g])),
            pw_send.at[g],
            pw_recv.at[g],
            mate,
        )

    for g in range(4):
        pw_copy(g).start()

    own_half = pl.ds(pl.multiple_of(c * 256, 256), 256)

    def swap_in(src, buf, i):
        to_partner = remote(
            src, buf.at[pl.ds(pl.multiple_of(th * 256, 256), 256)], io_send.at[i], io_recv.at[i], partner
        )
        local = pltpu.make_async_copy(src, buf.at[own_half], io_loc.at[i])
        return to_partner, local

    def to_mate(buf, i):
        return remote(buf.at[own_half], buf.at[own_half], io_send.at[2 + i], io_recv.at[2 + i], mate)

    swaps = [swap_in(tok, X, 0), swap_in(cot, C, 1)]

    @pl.when(stays)
    def _():
        for a, b in swaps:
            b.start()

    @pl.when(jnp.logical_not(stays))
    def _():
        swaps[0][0].start()

    for g in range(4):
        W[g][th, x, z, yl, chip_rows(c), :] = pw[c, :, BASE[g] : BASE[g] + WIDTH[g]]

    def ag_block(g, i, p, coords, rows):
        colour, off, n = PIECES[g][i]
        order = ORDER[colour]
        known = order[:p]
        sel = []
        for axis in ("x", "z"):
            sel.append(pl.ds(0, 4) if axis in known else pl.ds(coords[axis], 1))
        if "y" in known:
            hs, ys = pl.ds(0, 2), pl.ds(0, 2)
        else:
            hs, ys = pl.ds(coords["y"] // 2, 1), pl.ds(coords["y"] % 2, 1)
        return W[g].at[hs, sel[0], sel[1], ys, rows, pl.ds(off, n)]

    def ag_copy(g, i, p, which):
        s = SLOT[g, i]
        axis = ORDER[PIECES[g][i][0]][p]
        at = me[axis]
        if which < 2:
            ref = ag_block(g, i, p, me, pl.ds(0, 32))
            to = nbr(axis, 1 if which == 0 else 3)
        elif which == 2:
            ref = ag_block(g, i, p, {**me, axis: (at + 3) % 4}, pl.ds(0, 16))
            to = nbr(axis, 1)
        else:
            ref = ag_block(g, i, p, {**me, axis: (at + 1) % 4}, pl.ds(16, 16))
            to = nbr(axis, 3)
        return remote(ref, ref, ag_send.at[s, p, which], ag_recv.at[s, p, which], to)

    def ag_step(g, step):
        if step == 0:
            pw_copy(g).wait()
        p, sub = divmod(step, 2)
        for i in range(len(PIECES[g])):
            if sub == 0:
                if p > 0:
                    ag_copy(g, i, p - 1, 2).wait_recv()
                    ag_copy(g, i, p - 1, 3).wait_recv()
                if p < 3:
                    ag_copy(g, i, p, 0).start()
                    ag_copy(g, i, p, 1).start()
            else:
                ag_copy(g, i, p, 0).wait_recv()
                ag_copy(g, i, p, 2).start()
                ag_copy(g, i, p, 1).wait_recv()
                ag_copy(g, i, p, 3).start()

    def ag_drain(g):
        for i in range(len(PIECES[g])):
            for p in range(3):
                for which in range(4):
                    ag_copy(g, i, p, which).wait_send()

    def wave(t):
        for g in range(4):
            if 0 <= t - g <= 6:
                ag_step(g, t - g)

    wave(0)
    wave(1)

    @pl.when(stays)
    def _():
        swaps[0][1].wait()
        swaps[1][1].wait()

    @pl.when(jnp.logical_not(stays))
    def _():
        swaps[0][0].wait()
        swaps[1][0].start()

    to_mate(X, 0).start()
    for t in range(2, 7):
        wave(t)
    to_mate(X, 0).wait()

    qkv_dst = (Q, K, V)
    lanes = lax.broadcasted_iota(jnp.int32, (1, 128), 1)

    def project(j, hh):
        w = W[0][hh, :, :, :, :, j * 256 : (j + 1) * 256].reshape(1024, 256)
        out = dot(X[...], w, 1, 0)
        if j != 1:
            row = 0 if j == 0 else 1
            start = pl.multiple_of(hh * 512 + c * 256, 256)
            out = out + vec[row : row + 1, pl.ds(start, 256)]
        out = out.astype(BF16)
        if j == 0:
            out = out * jnp.asarray(0.125, BF16)
        qkv_dst[j][:, pl.ds(pl.multiple_of(hh * 256, 256), 256)] = out

    def project_all(hh, carry):
        for j in range(3):
            project(j, hh)
        return carry

    lax.fori_loop(0, 2, project_all, 0)

    wave(7)

    def head_mask(j):
        return (lanes < 64) if j == 0 else (lanes >= 64)

    def only(v, j):
        return jnp.where(head_mask(j), v, jnp.zeros_like(v))

    def attend(p, carry):
        cols = pl.ds(pl.multiple_of(p * 128, 128), 128)
        k2 = K[:, cols]
        v2 = V[:, cols]
        for r in range(2):
            rows = slice(r * 256, (r + 1) * 256)
            q2 = Q[rows, cols]
            acc = None
            for j in range(2):
                s = dot(only(q2, j), k2, 1, 1)
                s = jnp.exp(s - jnp.max(s, axis=-1, keepdims=True))
                s = s * (1.0 / jnp.sum(s, axis=-1, keepdims=True))
                pr = s.astype(BF16)
                PR[p * 2 + j, rows, :] = pr
                o = dot(pr, only(v2, j), 1, 0)
                acc = o if acc is None else acc + o
            MX[rows, cols] = acc.astype(BF16)
        return carry

    lax.fori_loop(0, 4, attend, 0)
    wave(8)

    def ex_copy(e, dst, i):
        cols = pl.ds(pl.multiple_of(i * 256, 256), 256)
        return remote(S.at[:, cols], dst.at[:, cols], ex_send.at[e, i], ex_recv.at[e, i], mate)

    def out_part(i, carry):
        acc = None
        for hh in range(2):
            w = W[1][hh, i].reshape(256, 256)
            o = dot(MX[:, hh * 256 : (hh + 1) * 256], w, 1, 1)
            acc = o if acc is None else acc + o
        S[:, pl.ds(pl.multiple_of(i * 256, 256), 256)] = acc.astype(BF16)
        ex_copy(0, R1, i).start()
        return carry

    lax.fori_loop(0, 4, out_part, 0)
    wave(9)

    def ex_wait(e, dst):
        for i in range(4):
            ex_copy(e, dst, i).wait()

    ex_wait(0, R1)

    def mean(v):
        return jnp.sum(v, axis=-1, keepdims=True) * (1.0 / 1024)

    def ln1(i, carry):
        rows = pl.ds(pl.multiple_of(i * 32, 32), 32)
        r = X[rows].astype(F32) + (S[rows].astype(F32) + R1[rows].astype(F32)) + vec[2:3]
        cen = r - mean(r)
        inv = lax.rsqrt(mean(cen * cen) + EPS)
        n = cen * inv
        N1[rows] = n
        INV1[rows] = jnp.broadcast_to(inv, (32, 128))
        H[rows] = (n * vec[3:4] + vec[4:5]).astype(BF16)
        return carry

    lax.fori_loop(0, 16, ln1, 0)

    def up(i, carry):
        cols = pl.ds(pl.multiple_of(i * 256, 256), 256)
        for hh in range(2):
            w = W[2][hh, :, :, :, :, cols].reshape(1024, 256)
            u = dot(H[...], w, 1, 0)
            u = u + vec[pl.ds(5 + hh * 2 + c, 1), cols]
            e = 0.5 * (1.0 + lax.erf(u * ROOT_HALF))
            dst = pl.ds(pl.multiple_of(hh * 1024 + i * 256, 256), 256)
            ACT[:, dst] = (u * e).astype(BF16)
            SL[:, dst] = (e + u * jnp.exp(-0.5 * u * u) * INV_ROOT_TAU).astype(BF16)
        return carry

    lax.fori_loop(0, 4, up, 0)

    def down(i, carry):
        acc = None
        for hh in range(2):
            w = W[3][hh, i].reshape(256, 1024)
            o = dot(ACT[:, hh * 1024 : (hh + 1) * 1024], w, 1, 1)
            acc = o if acc is None else acc + o
        S[:, pl.ds(pl.multiple_of(i * 256, 256), 256)] = acc.astype(BF16)
        ex_copy(1, R2, i).start()
        return carry

    lax.fori_loop(0, 4, down, 0)

    @pl.when(jnp.logical_not(stays))
    def _():
        swaps[1][0].wait()

    to_mate(C, 1).start()
    for g in range(4):
        ag_drain(g)
    to_mate(C, 1).wait()
    ex_wait(1, R2)

    ACC[...] = jnp.zeros_like(ACC)

    def fold(v):
        return v[0:8] + v[8:16] + (v[16:24] + v[24:32])

    def ln2(i, carry):
        rows = pl.ds(pl.multiple_of(i * 32, 32), 32)
        hidden = N1[rows] * vec[3:4] + vec[4:5]
        r = hidden + (S[rows].astype(F32) + R2[rows].astype(F32)) + vec[9:10]
        cen = r - mean(r)
        inv = lax.rsqrt(mean(cen * cen) + EPS)
        n = cen * inv
        ENC[rows] = (n * vec[10:11] + vec[11:12]).astype(BF16)
        g = C[rows].astype(F32)
        ACC[1] += fold(g * n)
        ACC[2] += fold(g)
        sc = g * vec[10:11]
        gr = inv * (sc - mean(sc) - n * mean(sc * n))
        ACC[0] += fold(gr)
        GR[rows] = gr
        GD[rows] = gr.astype(BF16)
        return carry

    lax.fori_loop(0, 16, ln2, 0)

    enc_local = pltpu.make_async_copy(ENC.at[own_half], enc_out, io_loc.at[2])
    enc_remote = remote(ENC.at[own_half], enc_out, io_send.at[4], io_recv.at[4], partner)

    def rs_axis(g, i, p):
        return ORDER[PIECES[g][i][0]][2 - p]

    def rs_open(g, i, p):
        return ORDER[PIECES[g][i][0]][: 2 - p]

    def rs_base(g, i, p, coord):
        opened = rs_open(g, i, p)
        at = {**me, rs_axis(g, i, p): coord}
        zero = jnp.int32(0)
        base = (
            zero if "y" in opened else at["y"] // 2,
            zero if "x" in opened else at["x"],
            zero if "z" in opened else at["z"],
            zero if "y" in opened else at["y"] % 2,
        )
        return base, block_dims(opened)

    def rs_block(g, i, p, coord, rows):
        base, dims = rs_base(g, i, p, coord)
        _, off, n = PIECES[g][i]
        return G[g].at[
            pl.ds(base[0], dims[0]),
            pl.ds(base[1], dims[1]),
            pl.ds(base[2], dims[2]),
            pl.ds(base[3], dims[3]),
            rows,
            pl.ds(off, n),
        ]

    def rs_copy(g, i, p, which):
        s = SLOT[g, i]
        axis = rs_axis(g, i, p)
        at = me[axis]
        far = (at + 2) % 4
        lower, upper = (at + 3) % 4, (at + 1) % 4
        if which == 0:
            src, dst, to = rs_block(g, i, p, far, pl.ds(0, 16)), rs1[s * 3 + p].at[0], nbr(axis, 3)
        elif which == 1:
            src, dst, to = rs_block(g, i, p, far, pl.ds(16, 16)), rs1[s * 3 + p].at[1], nbr(axis, 1)
        elif which == 2:
            src, dst, to = rs_block(g, i, p, lower, pl.ds(0, 32)), rs2[s * 3 + p].at[0], nbr(axis, 3)
        else:
            src, dst, to = rs_block(g, i, p, upper, pl.ds(0, 32)), rs2[s * 3 + p].at[1], nbr(axis, 1)
        return remote(src, dst, rs_send.at[s, p, which], rs_recv.at[s, p, which], to)

    def unflatten(i, dims):
        out = []
        for d in reversed(dims):
            out.append(i % d if d > 1 else 0)
            i = i // d if d > 1 else i
        return tuple(reversed(out))

    def rs_mid(g, i, p, which):
        s = SLOT[g, i]
        _, off, n = PIECES[g][i]
        at = me[rs_axis(g, i, p)]
        coord = (at + 3) % 4 if which == 0 else (at + 1) % 4
        base, dims = rs_base(g, i, p, coord)
        rows = slice(which * 16, which * 16 + 16)
        buf = rs1[s * 3 + p]

        def one(k, carry):
            a = unflatten(k, dims)
            b = tuple(u + w for u, w in zip(base, a))
            total = G[g][(*b, rows, slice(off, off + n))].astype(F32) + buf[(which, *a)].astype(F32)
            G[g][(*b, rows, slice(off, off + n))] = total.astype(BF16)
            return carry

        lax.fori_loop(0, dims[0] * dims[1] * dims[2] * dims[3], one, 0)

    def rs_fin(g, i, p):
        s = SLOT[g, i]
        _, off, n = PIECES[g][i]
        base, dims = rs_base(g, i, p, me[rs_axis(g, i, p)])
        buf = rs2[s * 3 + p]

        def one(k, carry):
            a = unflatten(k, dims)
            b = tuple(u + w for u, w in zip(base, a))
            total = (
                G[g][(*b, slice(0, 32), slice(off, off + n))].astype(F32)
                + buf[(0, *a)].astype(F32)
                + buf[(1, *a)].astype(F32)
            )
            if p == 2:
                FIN[:, BASE[g] + off : BASE[g] + off + n] = total
            else:
                G[g][(*b, slice(0, 32), slice(off, off + n))] = total.astype(BF16)
            return carry

        if p == 2:
            one(0, 0)
        else:
            lax.fori_loop(0, dims[0] * dims[1] * dims[2] * dims[3], one, 0)

    def fin_copy(g):
        cols = pl.ds(BASE[g], WIDTH[g])
        return remote(
            FIN.at[chip_rows(1 - c), cols],
            gw_out.at[c, :, cols],
            fin_send.at[g],
            fin_recv.at[g],
            mate,
        )

    def rs_step(g, step):
        p, sub = divmod(step, 2)
        for i in range(len(PIECES[g])):
            if sub == 0:
                if p > 0:
                    rs_copy(g, i, p - 1, 2).wait()
                    rs_copy(g, i, p - 1, 3).wait()
                    rs_fin(g, i, p - 1)
                if p < 3:
                    rs_copy(g, i, p, 0).start()
                    rs_copy(g, i, p, 1).start()
            else:
                rs_copy(g, i, p, 0).wait()
                rs_mid(g, i, p, 0)
                rs_copy(g, i, p, 2).start()
                rs_copy(g, i, p, 1).wait()
                rs_mid(g, i, p, 1)
                rs_copy(g, i, p, 3).start()
        if step == 6:
            cols = slice(BASE[g], BASE[g] + WIDTH[g])
            gw_out[pl.ds(c, 1), :, cols] = FIN[chip_rows(c), cols].reshape(1, 16, WIDTH[g])
            fin_copy(g).start()

    def weight_grad(g, a_ref, sources):
        def one(i, carry):
            a = a_ref[:, pl.ds(pl.multiple_of(i * 256, 256), 256)]
            for hh in range(2):
                at = 0
                for ref, starts, n in sources:
                    o = dot(a, ref[:, starts[hh] : starts[hh] + n], 0, 0)
                    G[g][hh, i, :, :, :, at : at + n] = o.astype(BF16).reshape(4, 2, 32, n)
                    at += n
            return carry

        lax.fori_loop(0, 4, one, 0)

    weight_grad(3, GD, [(ACT, (0, 1024), 1024)])
    rs_step(3, 0)

    @pl.when(stays)
    def _():
        enc_local.start()

    @pl.when(jnp.logical_not(stays))
    def _():
        enc_remote.start()

    def grad_up(i, carry):
        cols = pl.ds(pl.multiple_of(i * 256, 256), 256)
        for hh in range(2):
            w = W[3][hh, :, :, :, :, cols].reshape(1024, 256)
            dst = pl.ds(pl.multiple_of(hh * 1024 + i * 256, 256), 256)
            gu = (dot(GD[...], w, 1, 0) * SL[:, dst].astype(F32)).astype(BF16)
            SL[:, dst] = gu
            SVA[0, pl.ds(x, 1), hh : hh + 1, cols] = jnp.sum(
                gu.astype(F32), axis=0, keepdims=True
            ).reshape(1, 1, 256)
        return carry

    lax.fori_loop(0, 4, grad_up, 0)

    def hidden_part(i, carry):
        acc = None
        for hh in range(2):
            w = W[2][hh, i].reshape(256, 1024)
            o = dot(SL[:, hh * 1024 : (hh + 1) * 1024], w, 1, 1)
            acc = o if acc is None else acc + o
        S[:, pl.ds(pl.multiple_of(i * 256, 256), 256)] = acc.astype(BF16)
        ex_copy(2, R3, i).start()
        return carry

    lax.fori_loop(0, 4, hidden_part, 0)
    weight_grad(2, H, [(SL, (0, 1024), 1024)])
    rs_step(2, 0)
    rs_step(3, 1)
    ex_wait(2, R3)

    def ln1_back(i, carry):
        rows = pl.ds(pl.multiple_of(i * 32, 32), 32)
        gh = GR[rows] + (S[rows].astype(F32) + R3[rows].astype(F32))
        n = N1[rows]
        ACC[3] += fold(gh * n)
        ACC[4] += fold(gh)
        sc = gh * vec[3:4]
        inv = INV1[rows][:, 0:1]
        gr = inv * (sc - mean(sc) - n * mean(sc * n))
        ACC[5] += fold(gr)
        GR[rows] = gr
        GD[rows] = gr.astype(BF16)
        return carry

    lax.fori_loop(0, 16, ln1_back, 0)
    for i in range(6):
        SVA[0, pl.ds(x, 1), 2 + i : 3 + i, :] = jnp.sum(ACC[i], axis=0, keepdims=True).reshape(1, 1, 1024)

    SM_AXES = ("x", "z", "y")

    def sm_copy(buf, b, p, d):
        axis = SM_AXES[p]
        ref = buf.at[p, me[axis]]
        return remote(ref, ref, sm_send.at[b, p, d - 1], sm_recv.at[b, p, d - 1], nbr(axis, d))

    def sm_start(buf, b, p):
        for d in (1, 2, 3):
            sm_copy(buf, b, p, d).start()

    def sm_fin(buf, b, p, last):
        for d in (1, 2, 3):
            sm_copy(buf, b, p, d).wait()
        total = (buf[p, 0] + buf[p, 1]) + (buf[p, 2] + buf[p, 3])
        if p < 2:
            buf[p + 1, pl.ds(me[SM_AXES[p + 1]], 1)] = total.reshape(1, *total.shape)
        else:
            last[0] = total

    def smx_copy(ex, b):
        return remote(ex.at[0], ex.at[1], smx_send.at[b], smx_recv.at[b], mate)

    sm_start(SVA, 0, 0)

    for hh in range(2):
        w = W[1][hh].reshape(1024, 256)
        GM[:, hh * 256 : (hh + 1) * 256] = dot(GD[...], w, 1, 0).astype(BF16)
    weight_grad(1, GD, [(MX, (0, 256), 256)])
    rs_step(1, 0)
    rs_step(3, 2)

    def attend_back(p, carry):
        cols = pl.ds(pl.multiple_of(p * 128, 128), 128)
        q2 = Q[:, cols]
        k2 = K[:, cols]
        v2 = V[:, cols]
        gm2 = GM[:, cols]
        dk = None
        dq = None
        dv = None
        for j in range(2):
            gmj = only(gm2, j)
            pr = PR[p * 2 + j]
            prf = pr.astype(F32)
            gp = dot(gmj, v2, 1, 1)
            row = jnp.sum(prf * gp, axis=-1, keepdims=True)
            ds = (prf * (gp - row)).astype(BF16)
            a = dot(ds, only(k2, j), 1, 0)
            b = dot(ds, only(q2, j), 0, 0)
            e = dot(pr, gmj, 0, 0)
            dq = a if dq is None else dq + a
            dk = b if dk is None else dk + b
            dv = e if dv is None else dv + e
        dq = (dq * 0.125).astype(BF16)
        dv = dv.astype(BF16)
        DQ[:, cols] = dq
        DK[:, cols] = dk.astype(BF16)
        DV[:, cols] = dv
        SVB[0, pl.ds(x, 1), pl.ds(p, 1), :] = jnp.sum(dq.astype(F32), axis=0, keepdims=True).reshape(1, 1, 128)
        SVB[0, pl.ds(x, 1), pl.ds(4 + p, 1), :] = jnp.sum(dv.astype(F32), axis=0, keepdims=True).reshape(1, 1, 128)
        return carry

    lax.fori_loop(0, 2, attend_back, 0)
    rs_step(2, 1)
    rs_step(3, 3)
    sm_fin(SVA, 0, 0, EXA)
    sm_start(SVA, 0, 1)
    lax.fori_loop(2, 4, attend_back, 0)

    weight_grad(0, X, [(DQ, (0, 256), 256), (DK, (0, 256), 256), (DV, (0, 256), 256)])
    rs_step(0, 0)
    sm_start(SVB, 1, 0)
    rs_step(1, 1)
    rs_step(2, 2)
    rs_step(3, 4)
    sm_fin(SVA, 0, 1, EXA)
    sm_start(SVA, 0, 2)

    other_half = pl.ds(pl.multiple_of((1 - c) * 256, 256), 256)

    def rows_part(i, carry):
        cols = pl.ds(pl.multiple_of(i * 256, 256), 256)
        acc = None
        for hh in range(2):
            for j, ref in enumerate((DQ, DK, DV)):
                w = W[0][hh, i, :, :, :, j * 256 : (j + 1) * 256].reshape(256, 256)
                o = dot(ref[:, hh * 256 : (hh + 1) * 256], w, 1, 1)
                acc = o if acc is None else acc + o
        S[:, cols] = acc.astype(BF16)
        return carry

    lax.fori_loop(0, 4, rows_part, 0)
    rows_copy = remote(S.at[other_half], R4, ex_send.at[3, 0], ex_recv.at[3, 0], mate)
    rows_copy.start()
    rows_copy.wait()

    def finish(i, carry):
        here = pl.ds(pl.multiple_of(c * 256 + i * 32, 32), 32)
        rows = pl.ds(pl.multiple_of(i * 32, 32), 32)
        total = GR[here] + (S[here].astype(F32) + R4[rows].astype(F32))
        gtok_out[rows] = total
        GTS[rows] = total.astype(BF16)
        return carry

    lax.fori_loop(0, 8, finish, 0)
    gt_remote = remote(GTS, GTR, io_send.at[5], io_recv.at[5], partner)

    @pl.when(jnp.logical_not(stays))
    def _():
        gt_remote.start()

    rs_step(0, 1)
    sm_fin(SVB, 1, 0, EXB)
    sm_start(SVB, 1, 1)
    rs_step(1, 2)
    rs_step(2, 3)
    rs_step(3, 5)
    sm_fin(SVA, 0, 2, EXA)
    smx_copy(EXA, 0).start()
    rs_step(0, 2)
    sm_fin(SVB, 1, 1, EXB)
    sm_start(SVB, 1, 2)
    rs_step(1, 3)
    rs_step(2, 4)
    rs_step(3, 6)
    rs_step(0, 3)
    rs_step(1, 4)
    rs_step(2, 5)
    sm_fin(SVB, 1, 2, EXB)
    smx_copy(EXB, 1).start()
    rs_step(0, 4)
    rs_step(1, 5)
    rs_step(2, 6)
    rs_step(0, 5)
    rs_step(1, 6)
    smx_copy(EXA, 0).wait()
    smx_copy(EXB, 1).wait()
    small_out[...] = jnp.zeros_like(small_out)
    first = c == 0
    own_a, oth_a = EXA[0], EXA[1]
    low_a = jnp.where(first, own_a, oth_a)
    high_a = jnp.where(first, oth_a, own_a)
    for hh in range(2):
        small_out[5 + 2 * hh : 6 + 2 * hh, :] = low_a[hh : hh + 1]
        small_out[6 + 2 * hh : 7 + 2 * hh, :] = high_a[hh : hh + 1]
    for src, dst in ((2, 9), (3, 10), (4, 11), (5, 3), (6, 4), (7, 2)):
        small_out[dst : dst + 1, :] = low_a[src : src + 1]
    own_b, oth_b = EXB[0], EXB[1]
    parts_b = (jnp.where(first, own_b, oth_b), jnp.where(first, oth_b, own_b))
    for j in range(2):
        for hh in range(2):
            for cc in range(2):
                for u in range(2):
                    col = hh * 512 + cc * 256 + u * 128
                    k = j * 4 + hh * 2 + u
                    small_out[j : j + 1, col : col + 128] = parts_b[cc][k : k + 1]
    rs_step(0, 6)

    @pl.when(stays)
    def _():
        enc_local.wait()

    @pl.when(jnp.logical_not(stays))
    def _():
        enc_remote.wait()
        gt_remote.wait()

        def widen(i, carry):
            rows = pl.ds(pl.multiple_of(i * 32, 32), 32)
            gtok_out[rows] = GTR[rows].astype(F32)
            return carry

        lax.fori_loop(0, 8, widen, 0)

    for g in range(4):
        fin_copy(g).wait()


def scratch_list():
    def vm(shape, dtype=BF16):
        return pltpu.VMEM(shape, dtype)

    def weights(n):
        return vm((2, 4, 4, 2, 32, n))

    out = [weights(n) for n in WIDTH] + [weights(1024)]
    out += [vm((512, 1024)), vm((512, 1024))]
    out += [vm((512, 512))] * 3
    out += [vm((8, 512, 512)), vm((512, 512))]
    out += [vm((512, 1024), F32), vm((512, 128), F32), vm((512, 1024))]
    out += [vm((512, 2048)), vm((512, 2048))]
    out += [vm((512, 1024), F32), vm((512, 1024))]
    out += [vm((512, 512)), vm((512, 1024)), vm((256, 1024))]
    out += [vm((512, 1024))] * 4 + [vm((256, 1024))]
    out += [vm((6, 8, 1024), F32), vm((3, 4, 8, 1024), F32), vm((3, 4, 8, 128), F32)]
    out += [vm((2, 8, 1024), F32), vm((2, 8, 128), F32), vm((32, 3072), F32)]
    for rows in (16, 32):
        for g, i in PIECE_LIST:
            colour, _, n = PIECES[g][i]
            for p in range(3):
                out.append(vm((2, *block_dims(ORDER[colour][: 2 - p]), rows, n)))
    dma = pltpu.SemaphoreType.DMA
    out += [dma((NP, 3, 4))] * 4
    out += [dma((4, 4)), dma((4, 4)), dma((6,)), dma((6,)), dma((3,))]
    out += [dma((2, 3, 3)), dma((2, 3, 3)), dma((2,)), dma((2,))]
    out += [dma((4,))] * 4
    return out


def body(
    tokens,
    w_qkv,
    b_qv,
    w_out,
    b_out,
    gain_attn,
    shift_attn,
    w_in,
    b_in,
    w_back,
    b_back,
    gain_ffn,
    shift_ffn,
    cotangent,
):
    def halves(m, n):
        return m.reshape(16, 2, n).transpose(1, 0, 2)

    qkv = w_qkv[0].reshape(16, 3, 2, 256).transpose(2, 0, 1, 3).reshape(2, 16, 768)
    packed = jnp.concatenate(
        [qkv, halves(w_out[0].T, 256), halves(w_in[0], 1024), halves(w_back[0].T, 1024)], axis=2
    )
    vec = jnp.concatenate(
        [
            b_qv.reshape(2, 1024),
            b_out,
            gain_attn,
            shift_attn,
            b_in.reshape(4, 1024),
            b_back,
            gain_ffn,
            shift_ffn,
            jnp.zeros((4, 1024), BF16),
        ],
        axis=0,
    ).astype(F32)
    vmem = pl.BlockSpec(memory_space=pltpu.VMEM)
    hbm = pl.BlockSpec(memory_space=pl.ANY)
    enc, gtok, gw, small = pl.pallas_call(
        kernel,
        out_shape=(
            jax.ShapeDtypeStruct((256, 1024), BF16),
            jax.ShapeDtypeStruct((256, 1024), F32),
            jax.ShapeDtypeStruct((2, 16, 3072), F32),
            jax.ShapeDtypeStruct((16, 1024), F32),
        ),
        in_specs=[vmem, hbm, hbm, vmem],
        out_specs=(hbm, vmem, vmem, vmem),
        scratch_shapes=scratch_list(),
        compiler_params=pltpu.CompilerParams(
            collective_id=0, has_side_effects=True, vmem_limit_bytes=60 * 1024 * 1024
        ),
        cost_estimate=pl.CostEstimate(
            flops=22_000_000_000, bytes_accessed=5_000_000, transcendentals=6_000_000
        ),
        name="encoder_layer",
    )(packed, tokens, cotangent, vec)

    def join(col, n):
        return gw[:, :, col : col + n].transpose(1, 0, 2).reshape(16, 2 * n)

    g_qkv = gw[:, :, :768].reshape(2, 16, 3, 256).transpose(1, 2, 0, 3).reshape(1, 16, 3, 512)
    return (
        enc,
        gtok,
        g_qkv,
        small[0:2].reshape(1, 2, 1024),
        join(768, 256).T[None],
        small[2:3],
        small[3:4],
        small[4:5],
        join(1024, 1024)[None],
        small[5:9].reshape(1, 4096),
        join(2048, 1024).T[None],
        small[9:10],
        small[10:11],
        small[11:12],
    )


def solution(mesh):
    in_specs = (
        P(("dp", "tensor"), None),
        P(None, "dp", None, "tensor"),
        P(),
        P(None, "tensor", "dp"),
        P(),
        P(),
        P(),
        P(None, "dp", "tensor"),
        P(),
        P(None, "tensor", "dp"),
        P(),
        P(),
        P(),
        P(("dp", "tensor"), None),
    )
    out_specs = (
        P(("dp", "tensor"), None),
        P(("dp", "tensor"), None),
        P(None, "dp", None, "tensor"),
        P(),
        P(None, "tensor", "dp"),
        P(),
        P(),
        P(),
        P(None, "dp", "tensor"),
        P(),
        P(None, "tensor", "dp"),
        P(),
        P(),
        P(),
    )
    return jax.shard_map(body, mesh=mesh, in_specs=in_specs, out_specs=out_specs, check_vma=False)
```

time: 2160 us -> 208 us (0.10)
  waiting for transfers between devices: 1950 us -> 0 us
  Pallas kernels: 0 us -> 190 us
  matrix products: 76.8 us -> 0 us
  blocking collectives: 66.2 us -> 0 us
    reduce_scatter x7 -> x0, waiting for transfers between devices: 949 us -> none  [the longest x1 298 us: body(): lax.psum_scatter(g_in, 'dp', scatter_dimension=0, tiled=True)]
    all_gather x8 -> x0, waiting for transfers between devices: 503 us -> none  [the longest x1 106 us: fetch_forward(): lax.all_gather(shards[0], 'dp', axis=0, tiled=True)]
    unnamed x17 -> x0, waiting for transfers between devices: 497 us -> none
    pallas_call x0 -> x1, Pallas kernels: none -> 190 us  [body(): pl.pallas_call(kernel, out_shape=(jax.ShapeDtypeStruct((256, 1024), BF16)...]
    dot_general x18 -> x0, matrix products: 76.8 us -> none  [the longest x1 7.74 us: body(): jnp.dot(hidden_rows, full_in, preferred_element_type=jnp.float32)]
    psum x1 -> x0, blocking collectives: 66.2 us -> none  [body(): lax.psum((widen(d_bias_qv, model_width, 1), d_bias_out, d_gain1, d_shift1...]
  transfers between devices with their start and end apart: 16 -> 0, of which waited for: 15 -> 0; matrix products, arithmetic and copies ran while one was open for 3% -> 0% of each run, Pallas kernels for 0% -> 0%
where the time goes in v1:
time: 208 us; the launch traced here: 207 us
  Pallas kernels  190 us (91%)
  local copies, waits for them, and re-layouts  14.2 us (7%)
  other arithmetic  2.1 us (1%)
    pallas_call x1, Pallas kernels, body(): pl.pallas_call(kernel, out_shape=(jax.ShapeDtypeStruct((256, 1024), BF16)...  190 us
    unnamed x34, local copies, waits for them, and re-layouts  6.98 us

profile of v1, /device:TPU:1, one launch (start us, length us, event | category | flops | bytes accessed | tf_op | source)
XLA Modules:
  0.0 207.4 jit_solution(7931236470388559092)
XLA Ops:
  0.7 0.8 reduce
  1.4 0.0 copy-start.10
  1.5 0.6 copy-done.9
  2.1 0.0 copy-done.10
  2.1 0.0 copy-done.11
  2.1 0.0 copy-done.12
  2.2 0.0 copy-done.7
  2.2 0.0 copy-done.8
  2.2 0.2 concatenate.7
  2.4 0.5 copy-done.6
  2.9 0.6 convert_element_type.3.refs_3_
  3.6 0.2 copy-done.5
  3.8 0.1 reshape.61
  3.9 0.8 copy-done.3
  4.7 0.8 copy-done.4
  5.5 0.7 pad_maximum_fusion.refs_0_
  6.2 190.3 %encoder_layer.1 = (bf16[256,1024]{1,0:T(8,128)(2,1)}, f32[256,1024]{1,0:T(8,128)}, f32[2,16,3072]{2,1,0:T(8,128)}, f32[16,1024]{1,0:T(8,128)}) custom-call(bf16[2,16,3072]{2,1,0:T(8,128)(2,1)} %pad_maximum_fusion.refs_0_, bf16[256,1024]{1,0:T(8,128)(2,1)} %refs_1_.1, bf16[256,1024]{1,0:T(8,128)(2,1)} %refs_2_.1, f32[16,1024]{1,0:T(8,128)} %convert_element_type.3.refs_3_), custom_call_target="tpu_custom_call" | custom-call | flops 22000001024 | bytes 5000000 | tf_op jit(solution)/shard_map/encoder_layer/pallas_call | solution.py:827
  196.5 1.4 slice_bitcast_fusion.4
  197.9 0.8 slice_bitcast_fusion.3
  198.7 1.5 fusion
  200.2 0.6 copy.49
  200.9 0.8 slice_bitcast_fusion.2
  201.6 0.6 copy.47
  202.2 0.9 slice.36
  203.2 0.7 copy.48
  203.8 0.1 reshape.66
  203.9 0.1 copy.41
  204.0 0.7 reshape.67
  204.7 0.1 copy.43
  204.8 0.8 broadcast_in_dim_reshape.3
  205.6 0.8 copy.60
  206.4 1.0 copy.61
  (26 shorter events, 0.2 us)
Async XLA Ops:
  0.6 0.9 copy-start.13
  1.4 0.7 copy-start.9
  1.4 0.7 copy-start.10
  1.4 0.7 copy-start.11
  1.5 0.7 copy-start.12
  1.5 0.7 copy-start.7
  1.5 0.7 copy-start.8
  2.2 0.7 copy-start.6
  2.9 0.8 copy-start.5
  3.8 0.8 copy-start.3
  4.7 0.8 copy-start.4
  196.5 6.7 %copy-start.2 = (f32[2,16,3072]{2,1,0:T(8,128)S(1)}, f32[2,16,3072]{2,1,0:T(8,128)}, u32[]{:S(2)}) copy-start(f32[2,16,3072]{2,1,0:T(8,128)} %get-tuple-element.20) | copy-start | bytes 1179652
  203.8 1.8 copy-start.1
  203.9 2.5 %copy-start = (f32[256,1024]{1,0:T(8,128)S(1)}, f32[256,1024]{1,0:T(8,128)}, u32[]{:S(2)}) copy-start(f32[256,1024]{1,0:T(8,128)} %get-tuple-element.45) | copy-start | bytes 3145732

commit v2 on v1

--- a/solution.py
+++ b/solution.py
@@ -16,8 +16,8 @@
 BASE = (0, 768, 1024, 2048)
 PIECES = (
     ((0, 0, 256), (1, 256, 256), (2, 512, 256)),
-    ((0, 0, 128), (2, 128, 128)),
-    ((0, 0, 384), (1, 384, 384), (2, 768, 256)),
+    ((1, 0, 128), (2, 128, 128)),
+    ((0, 0, 256), (1, 256, 384), (2, 640, 384)),
     ((0, 0, 256), (1, 256, 384), (2, 640, 384)),
 )
 ORDER = (("x", "z", "y"), ("z", "y", "x"), ("y", "x", "z"))
@@ -47,8 +47,12 @@
         del refs[:n]
         return out
 
-    pw, tok, cot, vec = take(4)
-    enc_out, gtok_out, gw_out, small_out = take(4)
+    tok, cot, *raw = take(6)
+    small_in = take(8)
+    enc_out, gtok_out = take(2)
+    gw_out = take(4)
+    small_out = take(8)
+    (vec,) = take(1)
     W = take(4)
     G = [None] * 4
     (G[3],) = take(1)
@@ -57,10 +61,10 @@
     DQ, DK, DV, GTS = Q, K, V, H.at[pl.ds(0, 256)]
     S, R1, R2, R3, R4 = take(5)
     ACC, SVA, SVB, EXA, EXB, FIN = take(6)
-    rs1 = take(NP * 3)
+    rs1 = take(NP)
     rs2 = take(NP * 3)
     (ag_send, ag_recv, rs_send, rs_recv, ex_send, ex_recv, io_send, io_recv, io_loc) = take(9)
-    (sm_send, sm_recv, smx_send, smx_recv, pw_send, pw_recv, fin_send, fin_recv) = take(8)
+    (sm_send, sm_recv, smx_send, smx_recv, pw_send, pw_recv, pw_loc, fin_send, fin_recv) = take(9)
 
     dp = lax.axis_index("dp")
     th = lax.axis_index("tensor")
@@ -105,18 +109,23 @@
     def own_slot(ref, rows, cols):
         return ref.at[th, x, z, yl, rows, cols]
 
-    def pw_copy(g):
-        cols = pl.ds(BASE[g], WIDTH[g])
-        return remote(
-            pw.at[1 - c, :, cols],
-            own_slot(W[g], chip_rows(c), pl.ds(0, WIDTH[g])),
-            pw_send.at[g],
-            pw_recv.at[g],
-            mate,
-        )
-
-    for g in range(4):
-        pw_copy(g).start()
+    RAW = [(0, j, j * 256, 256) for j in range(3)] + [(1, None, 0, 256), (2, None, 0, 1024), (3, None, 0, 1024)]
+
+    def pw_pair(k):
+        g, j, at, n = RAW[k]
+
+        def src(t):
+            cols = pl.ds(pl.multiple_of(t * n, n), n)
+            return raw[g].at[j, :, cols] if g == 0 else raw[g].at[:, cols]
+
+        dst = own_slot(W[g], chip_rows(c), pl.ds(at, n))
+        away = remote(src(1 - c), dst, pw_send.at[k], pw_recv.at[k], mate)
+        return away, pltpu.make_async_copy(src(c), dst, pw_loc.at[k])
+
+    pairs = [pw_pair(k) for k in range(6)]
+    for away, here in pairs:
+        away.start()
+        here.start()
 
     own_half = pl.ds(pl.multiple_of(c * 256, 256), 256)
 
@@ -140,9 +149,6 @@
     @pl.when(jnp.logical_not(stays))
     def _():
         swaps[0][0].start()
-
-    for g in range(4):
-        W[g][th, x, z, yl, chip_rows(c), :] = pw[c, :, BASE[g] : BASE[g] + WIDTH[g]]
 
     def ag_block(g, i, p, coords, rows):
         colour, off, n = PIECES[g][i]
@@ -161,9 +167,9 @@
         s = SLOT[g, i]
         axis = ORDER[PIECES[g][i][0]][p]
         at = me[axis]
-        if which < 2:
+        if which < 2 or p < 2:
             ref = ag_block(g, i, p, me, pl.ds(0, 32))
-            to = nbr(axis, 1 if which == 0 else 3)
+            to = nbr(axis, (1, 3, 2)[which])
         elif which == 2:
             ref = ag_block(g, i, p, {**me, axis: (at + 3) % 4}, pl.ds(0, 16))
             to = nbr(axis, 1)
@@ -172,37 +178,54 @@
             to = nbr(axis, 3)
         return remote(ref, ref, ag_send.at[s, p, which], ag_recv.at[s, p, which], to)
 
-    def ag_step(g, step):
-        if step == 0:
-            pw_copy(g).wait()
-        p, sub = divmod(step, 2)
+    def ag_start(g, p):
         for i in range(len(PIECES[g])):
-            if sub == 0:
-                if p > 0:
-                    ag_copy(g, i, p - 1, 2).wait_recv()
-                    ag_copy(g, i, p - 1, 3).wait_recv()
-                if p < 3:
-                    ag_copy(g, i, p, 0).start()
-                    ag_copy(g, i, p, 1).start()
-            else:
-                ag_copy(g, i, p, 0).wait_recv()
-                ag_copy(g, i, p, 2).start()
-                ag_copy(g, i, p, 1).wait_recv()
-                ag_copy(g, i, p, 3).start()
+            for which in range(3 if p < 2 else 2):
+                ag_copy(g, i, p, which).start()
+
+    def ag_arrive(g, p):
+        for i in range(len(PIECES[g])):
+            for which in range(3):
+                ag_copy(g, i, p, which).wait_recv()
+
+    def ag_forward(g):
+        for i in range(len(PIECES[g])):
+            ag_copy(g, i, 2, 0).wait_recv()
+            ag_copy(g, i, 2, 2).start()
+            ag_copy(g, i, 2, 1).wait_recv()
+            ag_copy(g, i, 2, 3).start()
+
+    def ag_finish(g):
+        for i in range(len(PIECES[g])):
+            ag_copy(g, i, 2, 2).wait_recv()
+            ag_copy(g, i, 2, 3).wait_recv()
 
     def ag_drain(g):
         for i in range(len(PIECES[g])):
             for p in range(3):
-                for which in range(4):
+                for which in range(3 if p < 2 else 4):
                     ag_copy(g, i, p, which).wait_send()
 
-    def wave(t):
+    for g in range(4):
+        for k in range(6):
+            if RAW[k][0] == g:
+                pairs[k][1].wait()
+                pairs[k][0].wait()
+        ag_start(g, 0)
+
+    for i, ref in zip((0, 2, 3, 4, 5, 9, 10, 11), small_in):
+        if i == 0:
+            vec[0:2] = ref[0].astype(F32)
+        elif i == 5:
+            for k in range(4):
+                vec[5 + k : 6 + k] = ref[:, k * 1024 : (k + 1) * 1024].astype(F32)
+        else:
+            vec[i : i + 1] = ref[...].astype(F32)
+
+    for p in range(2):
         for g in range(4):
-            if 0 <= t - g <= 6:
-                ag_step(g, t - g)
-
-    wave(0)
-    wave(1)
+            ag_arrive(g, p)
+            ag_start(g, p + 1)
 
     @pl.when(stays)
     def _():
@@ -215,9 +238,10 @@
         swaps[1][0].start()
 
     to_mate(X, 0).start()
-    for t in range(2, 7):
-        wave(t)
+    ag_forward(0)
+    ag_forward(1)
     to_mate(X, 0).wait()
+    ag_finish(0)
 
     qkv_dst = (Q, K, V)
     lanes = lax.broadcasted_iota(jnp.int32, (1, 128), 1)
@@ -240,8 +264,7 @@
         return carry
 
     lax.fori_loop(0, 2, project_all, 0)
-
-    wave(7)
+    ag_forward(2)
 
     def head_mask(j):
         return (lanes < 64) if j == 0 else (lanes >= 64)
@@ -269,7 +292,7 @@
         return carry
 
     lax.fori_loop(0, 4, attend, 0)
-    wave(8)
+    ag_finish(1)
 
     def ex_copy(e, dst, i):
         cols = pl.ds(pl.multiple_of(i * 256, 256), 256)
@@ -286,7 +309,7 @@
         return carry
 
     lax.fori_loop(0, 4, out_part, 0)
-    wave(9)
+    ag_forward(3)
 
     def ex_wait(e, dst):
         for i in range(4):
@@ -308,7 +331,8 @@
         H[rows] = (n * vec[3:4] + vec[4:5]).astype(BF16)
         return carry
 
-    lax.fori_loop(0, 16, ln1, 0)
+    lax.fori_loop(0, 16, ln1, 0, unroll=2)
+    ag_finish(2)
 
     def up(i, carry):
         cols = pl.ds(pl.multiple_of(i * 256, 256), 256)
@@ -324,6 +348,13 @@
 
     lax.fori_loop(0, 4, up, 0)
 
+    @pl.when(jnp.logical_not(stays))
+    def _():
+        swaps[1][0].wait()
+
+    to_mate(C, 1).start()
+    ag_finish(3)
+
     def down(i, carry):
         acc = None
         for hh in range(2):
@@ -336,11 +367,6 @@
 
     lax.fori_loop(0, 4, down, 0)
 
-    @pl.when(jnp.logical_not(stays))
-    def _():
-        swaps[1][0].wait()
-
-    to_mate(C, 1).start()
     for g in range(4):
         ag_drain(g)
     to_mate(C, 1).wait()
@@ -369,7 +395,7 @@
         GD[rows] = gr.astype(BF16)
         return carry
 
-    lax.fori_loop(0, 16, ln2, 0)
+    lax.fori_loop(0, 16, ln2, 0, unroll=2)
 
     enc_local = pltpu.make_async_copy(ENC.at[own_half], enc_out, io_loc.at[2])
     enc_remote = remote(ENC.at[own_half], enc_out, io_send.at[4], io_recv.at[4], partner)
@@ -410,14 +436,16 @@
         at = me[axis]
         far = (at + 2) % 4
         lower, upper = (at + 3) % 4, (at + 1) % 4
-        if which == 0:
-            src, dst, to = rs_block(g, i, p, far, pl.ds(0, 16)), rs1[s * 3 + p].at[0], nbr(axis, 3)
-        elif which == 1:
-            src, dst, to = rs_block(g, i, p, far, pl.ds(16, 16)), rs1[s * 3 + p].at[1], nbr(axis, 1)
+        if p == 0 and which == 0:
+            src, dst, to = rs_block(g, i, p, far, pl.ds(0, 16)), rs1[s].at[0], nbr(axis, 3)
+        elif p == 0 and which == 1:
+            src, dst, to = rs_block(g, i, p, far, pl.ds(16, 16)), rs1[s].at[1], nbr(axis, 1)
         elif which == 2:
             src, dst, to = rs_block(g, i, p, lower, pl.ds(0, 32)), rs2[s * 3 + p].at[0], nbr(axis, 3)
+        elif which == 3:
+            src, dst, to = rs_block(g, i, p, upper, pl.ds(0, 32)), rs2[s * 3 + p].at[1], nbr(axis, 1)
         else:
-            src, dst, to = rs_block(g, i, p, upper, pl.ds(0, 32)), rs2[s * 3 + p].at[1], nbr(axis, 1)
+            src, dst, to = rs_block(g, i, p, far, pl.ds(0, 32)), rs2[s * 3 + p].at[2], nbr(axis, 2)
         return remote(src, dst, rs_send.at[s, p, which], rs_recv.at[s, p, which], to)
 
     def unflatten(i, dims):
@@ -434,7 +462,7 @@
         coord = (at + 3) % 4 if which == 0 else (at + 1) % 4
         base, dims = rs_base(g, i, p, coord)
         rows = slice(which * 16, which * 16 + 16)
-        buf = rs1[s * 3 + p]
+        buf = rs1[s]
 
         def one(k, carry):
             a = unflatten(k, dims)
@@ -459,6 +487,8 @@
                 + buf[(0, *a)].astype(F32)
                 + buf[(1, *a)].astype(F32)
             )
+            if p > 0:
+                total = total + buf[(2, *a)].astype(F32)
             if p == 2:
                 FIN[:, BASE[g] + off : BASE[g] + off + n] = total
             else:
@@ -470,38 +500,51 @@
         else:
             lax.fori_loop(0, dims[0] * dims[1] * dims[2] * dims[3], one, 0)
 
-    def fin_copy(g):
-        cols = pl.ds(BASE[g], WIDTH[g])
-        return remote(
-            FIN.at[chip_rows(1 - c), cols],
-            gw_out.at[c, :, cols],
-            fin_send.at[g],
-            fin_recv.at[g],
-            mate,
+    def fin_pair(k):
+        g, j, at, n = RAW[k]
+        cols = pl.ds(pl.multiple_of(c * n, n), n)
+        dst = gw_out[g].at[j, :, cols] if g == 0 else gw_out[g].at[:, cols]
+        src = slice(BASE[g] + at, BASE[g] + at + n)
+
+        def keep():
+            mine = FIN[chip_rows(c), src]
+            if g == 0:
+                gw_out[g][j, :, cols] = mine
+            else:
+                gw_out[g][:, cols] = mine
+
+        away = remote(
+            FIN.at[chip_rows(1 - c), pl.ds(BASE[g] + at, n)], dst, fin_send.at[k], fin_recv.at[k], mate
         )
+        return away, keep
+
+    fins = [fin_pair(k) for k in range(6)]
 
     def rs_step(g, step):
-        p, sub = divmod(step, 2)
         for i in range(len(PIECES[g])):
-            if sub == 0:
-                if p > 0:
-                    rs_copy(g, i, p - 1, 2).wait()
-                    rs_copy(g, i, p - 1, 3).wait()
-                    rs_fin(g, i, p - 1)
-                if p < 3:
-                    rs_copy(g, i, p, 0).start()
-                    rs_copy(g, i, p, 1).start()
+            if step == 0:
+                rs_copy(g, i, 0, 0).start()
+                rs_copy(g, i, 0, 1).start()
+            elif step == 1:
+                rs_copy(g, i, 0, 0).wait()
+                rs_mid(g, i, 0, 0)
+                rs_copy(g, i, 0, 2).start()
+                rs_copy(g, i, 0, 1).wait()
+                rs_mid(g, i, 0, 1)
+                rs_copy(g, i, 0, 3).start()
             else:
-                rs_copy(g, i, p, 0).wait()
-                rs_mid(g, i, p, 0)
-                rs_copy(g, i, p, 2).start()
-                rs_copy(g, i, p, 1).wait()
-                rs_mid(g, i, p, 1)
-                rs_copy(g, i, p, 3).start()
-        if step == 6:
-            cols = slice(BASE[g], BASE[g] + WIDTH[g])
-            gw_out[pl.ds(c, 1), :, cols] = FIN[chip_rows(c), cols].reshape(1, 16, WIDTH[g])
-            fin_copy(g).start()
+                p = step - 2
+                for which in (2, 3) if p == 0 else (2, 3, 4):
+                    rs_copy(g, i, p, which).wait()
+                rs_fin(g, i, p)
+                if p < 2:
+                    for which in (2, 3, 4):
+                        rs_copy(g, i, p + 1, which).start()
+        if step == 4:
+            for k in range(6):
+                if RAW[k][0] == g:
+                    fins[k][0].start()
+                    fins[k][1]()
 
     def weight_grad(g, a_ref, sources):
         def one(i, carry):
@@ -571,7 +614,7 @@
         GD[rows] = gr.astype(BF16)
         return carry
 
-    lax.fori_loop(0, 16, ln1_back, 0)
+    lax.fori_loop(0, 16, ln1_back, 0, unroll=2)
     for i in range(6):
         SVA[0, pl.ds(x, 1), 2 + i : 3 + i, :] = jnp.sum(ACC[i], axis=0, keepdims=True).reshape(1, 1, 1024)
 
@@ -605,7 +648,6 @@
         GM[:, hh * 256 : (hh + 1) * 256] = dot(GD[...], w, 1, 0).astype(BF16)
     weight_grad(1, GD, [(MX, (0, 256), 256)])
     rs_step(1, 0)
-    rs_step(3, 2)
 
     def attend_back(p, carry):
         cols = pl.ds(pl.multiple_of(p * 128, 128), 128)
@@ -640,7 +682,6 @@
 
     lax.fori_loop(0, 2, attend_back, 0)
     rs_step(2, 1)
-    rs_step(3, 3)
     sm_fin(SVA, 0, 0, EXA)
     sm_start(SVA, 0, 1)
     lax.fori_loop(2, 4, attend_back, 0)
@@ -648,11 +689,6 @@
     weight_grad(0, X, [(DQ, (0, 256), 256), (DK, (0, 256), 256), (DV, (0, 256), 256)])
     rs_step(0, 0)
     sm_start(SVB, 1, 0)
-    rs_step(1, 1)
-    rs_step(2, 2)
-    rs_step(3, 4)
-    sm_fin(SVA, 0, 1, EXA)
-    sm_start(SVA, 0, 2)
 
     other_half = pl.ds(pl.multiple_of((1 - c) * 256, 256), 256)
 
@@ -670,6 +706,10 @@
     lax.fori_loop(0, 4, rows_part, 0)
     rows_copy = remote(S.at[other_half], R4, ex_send.at[3, 0], ex_recv.at[3, 0], mate)
     rows_copy.start()
+    rs_step(1, 1)
+    rs_step(3, 2)
+    sm_fin(SVA, 0, 1, EXA)
+    sm_start(SVA, 0, 2)
     rows_copy.wait()
 
     def finish(i, carry):
@@ -690,39 +730,34 @@
     rs_step(0, 1)
     sm_fin(SVB, 1, 0, EXB)
     sm_start(SVB, 1, 1)
+    rs_step(2, 2)
     rs_step(1, 2)
-    rs_step(2, 3)
-    rs_step(3, 5)
+    rs_step(3, 3)
     sm_fin(SVA, 0, 2, EXA)
     smx_copy(EXA, 0).start()
     rs_step(0, 2)
     sm_fin(SVB, 1, 1, EXB)
     sm_start(SVB, 1, 2)
+    rs_step(2, 3)
     rs_step(1, 3)
-    rs_step(2, 4)
-    rs_step(3, 6)
+    rs_step(3, 4)
     rs_step(0, 3)
-    rs_step(1, 4)
-    rs_step(2, 5)
     sm_fin(SVB, 1, 2, EXB)
     smx_copy(EXB, 1).start()
-    rs_step(0, 4)
-    rs_step(1, 5)
-    rs_step(2, 6)
-    rs_step(0, 5)
-    rs_step(1, 6)
+    rs_step(2, 4)
+    rs_step(1, 4)
     smx_copy(EXA, 0).wait()
     smx_copy(EXB, 1).wait()
-    small_out[...] = jnp.zeros_like(small_out)
+    o_bqv, o_bout, o_ga, o_sa, o_bin, o_bb, o_gf, o_sf = small_out
     first = c == 0
     own_a, oth_a = EXA[0], EXA[1]
     low_a = jnp.where(first, own_a, oth_a)
     high_a = jnp.where(first, oth_a, own_a)
     for hh in range(2):
-        small_out[5 + 2 * hh : 6 + 2 * hh, :] = low_a[hh : hh + 1]
-        small_out[6 + 2 * hh : 7 + 2 * hh, :] = high_a[hh : hh + 1]
-    for src, dst in ((2, 9), (3, 10), (4, 11), (5, 3), (6, 4), (7, 2)):
-        small_out[dst : dst + 1, :] = low_a[src : src + 1]
+        o_bin[:, hh * 2048 : hh * 2048 + 1024] = low_a[hh : hh + 1]
+        o_bin[:, hh * 2048 + 1024 : hh * 2048 + 2048] = high_a[hh : hh + 1]
+    for src, dst in ((2, o_bb), (3, o_gf), (4, o_sf), (5, o_ga), (6, o_sa), (7, o_bout)):
+        dst[...] = low_a[src : src + 1]
     own_b, oth_b = EXB[0], EXB[1]
     parts_b = (jnp.where(first, own_b, oth_b), jnp.where(first, oth_b, own_b))
     for j in range(2):
@@ -731,8 +766,8 @@
                 for u in range(2):
                     col = hh * 512 + cc * 256 + u * 128
                     k = j * 4 + hh * 2 + u
-                    small_out[j : j + 1, col : col + 128] = parts_b[cc][k : k + 1]
-    rs_step(0, 6)
+                    o_bqv[0, j : j + 1, col : col + 128] = parts_b[cc][k : k + 1]
+    rs_step(0, 4)
 
     @pl.when(stays)
     def _():
@@ -750,8 +785,8 @@
 
         lax.fori_loop(0, 8, widen, 0)
 
-    for g in range(4):
-        fin_copy(g).wait()
+    for away, _ in fins:
+        away.wait()
 
 
 def scratch_list():
@@ -761,7 +796,7 @@
     def weights(n):
         return vm((2, 4, 4, 2, 32, n))
 
-    out = [weights(n) for n in WIDTH] + [weights(1024)]
+    out = [vm((16, 1024), F32)] + [weights(n) for n in WIDTH] + [weights(1024)]
     out += [vm((512, 1024)), vm((512, 1024))]
     out += [vm((512, 512))] * 3
     out += [vm((8, 512, 512)), vm((512, 512))]
@@ -772,16 +807,18 @@
     out += [vm((512, 1024))] * 4 + [vm((256, 1024))]
     out += [vm((6, 8, 1024), F32), vm((3, 4, 8, 1024), F32), vm((3, 4, 8, 128), F32)]
     out += [vm((2, 8, 1024), F32), vm((2, 8, 128), F32), vm((32, 3072), F32)]
-    for rows in (16, 32):
-        for g, i in PIECE_LIST:
-            colour, _, n = PIECES[g][i]
-            for p in range(3):
-                out.append(vm((2, *block_dims(ORDER[colour][: 2 - p]), rows, n)))
+    for g, i in PIECE_LIST:
+        colour, _, n = PIECES[g][i]
+        out.append(vm((2, *block_dims(ORDER[colour][:2]), 16, n)))
+    for g, i in PIECE_LIST:
+        colour, _, n = PIECES[g][i]
+        for p in range(3):
+            out.append(vm((2 if p == 0 else 3, *block_dims(ORDER[colour][: 2 - p]), 32, n)))
     dma = pltpu.SemaphoreType.DMA
-    out += [dma((NP, 3, 4))] * 4
+    out += [dma((NP, 3, 4))] * 2 + [dma((NP, 3, 5))] * 2
     out += [dma((4, 4)), dma((4, 4)), dma((6,)), dma((6,)), dma((3,))]
     out += [dma((2, 3, 3)), dma((2, 3, 3)), dma((2,)), dma((2,))]
-    out += [dma((4,))] * 4
+    out += [dma((6,))] * 5
     return out
 
 
@@ -801,39 +838,25 @@
     shift_ffn,
     cotangent,
 ):
-    def halves(m, n):
-        return m.reshape(16, 2, n).transpose(1, 0, 2)
-
-    qkv = w_qkv[0].reshape(16, 3, 2, 256).transpose(2, 0, 1, 3).reshape(2, 16, 768)
-    packed = jnp.concatenate(
-        [qkv, halves(w_out[0].T, 256), halves(w_in[0], 1024), halves(w_back[0].T, 1024)], axis=2
-    )
-    vec = jnp.concatenate(
-        [
-            b_qv.reshape(2, 1024),
-            b_out,
-            gain_attn,
-            shift_attn,
-            b_in.reshape(4, 1024),
-            b_back,
-            gain_ffn,
-            shift_ffn,
-            jnp.zeros((4, 1024), BF16),
-        ],
-        axis=0,
-    ).astype(F32)
     vmem = pl.BlockSpec(memory_space=pltpu.VMEM)
     hbm = pl.BlockSpec(memory_space=pl.ANY)
-    enc, gtok, gw, small = pl.pallas_call(
+    shapes = (
+        jax.ShapeDtypeStruct((256, 1024), BF16),
+        jax.ShapeDtypeStruct((256, 1024), F32),
+        jax.ShapeDtypeStruct((3, 16, 512), F32),
+        jax.ShapeDtypeStruct((16, 512), F32),
+        jax.ShapeDtypeStruct((16, 2048), F32),
+        jax.ShapeDtypeStruct((16, 2048), F32),
+        jax.ShapeDtypeStruct((1, 2, 1024), F32),
+        *(jax.ShapeDtypeStruct((1, 1024), F32) for _ in range(3)),
+        jax.ShapeDtypeStruct((1, 4096), F32),
+        *(jax.ShapeDtypeStruct((1, 1024), F32) for _ in range(3)),
+    )
+    results = pl.pallas_call(
         kernel,
-        out_shape=(
-            jax.ShapeDtypeStruct((256, 1024), BF16),
-            jax.ShapeDtypeStruct((256, 1024), F32),
-            jax.ShapeDtypeStruct((2, 16, 3072), F32),
-            jax.ShapeDtypeStruct((16, 1024), F32),
-        ),
-        in_specs=[vmem, hbm, hbm, vmem],
-        out_specs=(hbm, vmem, vmem, vmem),
+        out_shape=shapes,
+        in_specs=[hbm] * 6 + [vmem] * 8,
+        out_specs=(hbm, *[vmem] * 13),
         scratch_shapes=scratch_list(),
         compiler_params=pltpu.CompilerParams(
             collective_id=0, has_side_effects=True, vmem_limit_bytes=60 * 1024 * 1024
@@ -842,27 +865,59 @@
             flops=22_000_000_000, bytes_accessed=5_000_000, transcendentals=6_000_000
         ),
         name="encoder_layer",
-    )(packed, tokens, cotangent, vec)
-
-    def join(col, n):
-        return gw[:, :, col : col + n].transpose(1, 0, 2).reshape(16, 2 * n)
-
-    g_qkv = gw[:, :, :768].reshape(2, 16, 3, 256).transpose(1, 2, 0, 3).reshape(1, 16, 3, 512)
+    )(
+        tokens,
+        cotangent,
+        w_qkv[0].transpose(1, 0, 2),
+        w_out[0].T,
+        w_in[0],
+        w_back[0].T,
+        b_qv,
+        b_out,
+        gain_attn,
+        shift_attn,
+        b_in,
+        b_back,
+        gain_ffn,
+        shift_ffn,
+    )
+
+    def hand_on(*refs):
+        n = len(shapes)
+        ins, outs, bufs, sems = refs[:n], refs[n : 2 * n], refs[2 * n : 3 * n], refs[3 * n]
+        loads = [pltpu.make_async_copy(ins[i], bufs[i], sems.at[0, i]) for i in range(n)]
+        stores = [pltpu.make_async_copy(bufs[i], outs[i], sems.at[1, i]) for i in range(n)]
+        for load in loads:
+            load.start()
+        for load, store in zip(loads, stores):
+            load.wait()
+            store.start()
+        for store in stores:
+            store.wait()
+
+    enc, gtok, gq, go, gi, gb, d_bqv, d_bout, d_ga, d_sa, d_bin, d_bb, d_gf, d_sf = pl.pallas_call(
+        hand_on,
+        out_shape=shapes,
+        in_specs=[hbm] * 14,
+        out_specs=(hbm,) * 14,
+        scratch_shapes=[*(pltpu.VMEM(t.shape, t.dtype) for t in shapes), pltpu.SemaphoreType.DMA((2, 14))],
+        name="hand_on",
+    )(*results)
     return (
         enc,
         gtok,
-        g_qkv,
-        small[0:2].reshape(1, 2, 1024),
-        join(768, 256).T[None],
-        small[2:3],
-        small[3:4],
-        small[4:5],
-        join(1024, 1024)[None],
-        small[5:9].reshape(1, 4096),
-        join(2048, 1024).T[None],
-        small[9:10],
-        small[10:11],
-        small[11:12],
+        gq.transpose(1, 0, 2)[None],
+        d_bqv,
+        go.T[None],
+        d_bout,
+        d_ga,
+        d_sa,
+        gi[None],
+        d_bin,
+        gb.T[None],
+        d_bb,
+        d_gf,
+        d_sf,
     )
 
 

time: 208 us -> 173 us (0.83)
  Pallas kernels: 190 us -> 172 us
  local copies, waits for them, and re-layouts: 14.2 us -> 0 us
  other arithmetic: 2.1 us -> 0 us
    pallas_call x1 -> x2, Pallas kernels: 190 us -> 172 us  [the longest x1 169 us: body(): pl.pallas_call(kernel, out_shape=shapes, in_specs=[hbm] * 6 + [vmem] * 8,...]
    unnamed x34 -> x0, local copies, waits for them, and re-layouts: 6.98 us -> none
    reshape x9 -> x0, local copies, waits for them, and re-layouts: 3.55 us -> none  [the longest x1 1.41 us: body(): small[0:2].reshape(1, 2, 1024)]
    slice x2 -> x0, local copies, waits for them, and re-layouts: 2.4 us -> none  [the longest x1 1.5 us: body(): small[11:12]]
where the time goes in v2:
time: 173 us
  Pallas kernels  172 us (99%)
    pallas_call x1, Pallas kernels, body(): pl.pallas_call(kernel, out_shape=shapes, in_specs=[hbm] * 6 + [vmem] * 8,...  169 us

profile of v2, /device:TPU:1, one launch (start us, length us, event | category | flops | bytes accessed | tf_op | source)
XLA Modules:
  0.0 172.5 jit_solution(2842493272886448476)
XLA Ops:
  0.7 169.0 %encoder_layer.1 = (bf16[256,1024]{1,0:T(8,128)(2,1)}, f32[256,1024]{1,0:T(8,128)}, f32[3,16,512]{2,1,0:T(8,128)}, f32[16,512]{1,0:T(8,128)}, f32[16,2048]{1,0:T...) custom-call(bf16[256,1024]{1,0:T(8,128)(2,1)} %refs_0_.1, ...), custom_call_target="tpu_custom_call" | custom-call | flops 22000001024 | bytes 5000000 | tf_op jit(solution)/shard_map/encoder_layer/pallas_call | solution.py:855
  169.6 2.7 %hand_on.1 = (bf16[256,1024]{1,0:T(8,128)(2,1)}, f32[256,1024]{1,0:T(8,128)}, f32[3,16,512]{2,1,0:T(8,128)}, f32[16,512]{1,0:T(8,128)}, f32[16,2048]{1,0:T(8,128...) custom-call(bf16[256,1024]{1,0:T(8,128)(2,1)} %get-tuple-element.42., ...), custom_call_target="tpu_custom_call" | custom-call | tf_op jit(solution)/shard_map/hand_on/pallas_call | solution.py:898

commit v3 on v2

--- a/solution.py
+++ b/solution.py
@@ -17,8 +17,8 @@
 PIECES = (
     ((0, 0, 256), (1, 256, 256), (2, 512, 256)),
     ((1, 0, 128), (2, 128, 128)),
-    ((0, 0, 256), (1, 256, 384), (2, 640, 384)),
-    ((0, 0, 256), (1, 256, 384), (2, 640, 384)),
+    ((0, 0, 384), (1, 384, 384), (2, 768, 256)),
+    ((0, 0, 384), (1, 384, 256), (2, 640, 384)),
 )
 ORDER = (("x", "z", "y"), ("z", "y", "x"), ("y", "x", "z"))
 PIECE_LIST = [(g, i) for g in range(4) for i in range(len(PIECES[g]))]
@@ -141,15 +141,6 @@
 
     swaps = [swap_in(tok, X, 0), swap_in(cot, C, 1)]
 
-    @pl.when(stays)
-    def _():
-        for a, b in swaps:
-            b.start()
-
-    @pl.when(jnp.logical_not(stays))
-    def _():
-        swaps[0][0].start()
-
     def ag_block(g, i, p, coords, rows):
         colour, off, n = PIECES[g][i]
         order = ORDER[colour]
@@ -213,6 +204,15 @@
                 pairs[k][0].wait()
         ag_start(g, 0)
 
+    @pl.when(stays)
+    def _():
+        for a, b in swaps:
+            b.start()
+
+    @pl.when(jnp.logical_not(stays))
+    def _():
+        swaps[0][0].start()
+
     for i, ref in zip((0, 2, 3, 4, 5, 9, 10, 11), small_in):
         if i == 0:
             vec[0:2] = ref[0].astype(F32)
@@ -222,10 +222,12 @@
         else:
             vec[i : i + 1] = ref[...].astype(F32)
 
-    for p in range(2):
-        for g in range(4):
-            ag_arrive(g, p)
-            ag_start(g, p + 1)
+    for g in range(4):
+        ag_arrive(g, 0)
+        ag_start(g, 1)
+    for g in range(2):
+        ag_arrive(g, 1)
+        ag_start(g, 2)
 
     @pl.when(stays)
     def _():
@@ -239,6 +241,8 @@
 
     to_mate(X, 0).start()
     ag_forward(0)
+    ag_arrive(2, 1)
+    ag_start(2, 2)
     ag_forward(1)
     to_mate(X, 0).wait()
     ag_finish(0)
@@ -264,6 +268,8 @@
         return carry
 
     lax.fori_loop(0, 2, project_all, 0)
+    ag_arrive(3, 1)
+    ag_start(3, 2)
     ag_forward(2)
 
     def head_mask(j):
@@ -595,9 +601,9 @@
         return carry
 
     lax.fori_loop(0, 4, hidden_part, 0)
+    rs_step(3, 1)
     weight_grad(2, H, [(SL, (0, 1024), 1024)])
     rs_step(2, 0)
-    rs_step(3, 1)
     ex_wait(2, R3)
 
     def ln1_back(i, carry):
@@ -685,9 +691,11 @@
     sm_fin(SVA, 0, 0, EXA)
     sm_start(SVA, 0, 1)
     lax.fori_loop(2, 4, attend_back, 0)
-
     weight_grad(0, X, [(DQ, (0, 256), 256), (DK, (0, 256), 256), (DV, (0, 256), 256)])
     rs_step(0, 0)
+    rs_step(1, 1)
+    rs_step(3, 2)
+
     sm_start(SVB, 1, 0)
 
     other_half = pl.ds(pl.multiple_of((1 - c) * 256, 256), 256)
@@ -706,10 +714,9 @@
     lax.fori_loop(0, 4, rows_part, 0)
     rows_copy = remote(S.at[other_half], R4, ex_send.at[3, 0], ex_recv.at[3, 0], mate)
     rows_copy.start()
-    rs_step(1, 1)
-    rs_step(3, 2)
     sm_fin(SVA, 0, 1, EXA)
     sm_start(SVA, 0, 2)
+    rs_step(0, 1)
     rows_copy.wait()
 
     def finish(i, carry):
@@ -727,7 +734,6 @@
     def _():
         gt_remote.start()
 
-    rs_step(0, 1)
     sm_fin(SVB, 1, 0, EXB)
     sm_start(SVB, 1, 1)
     rs_step(2, 2)

time: 173 us -> 164 us (0.948)
  Pallas kernels: 172 us -> 163 us
    pallas_call x1, Pallas kernels: 169 us -> 160 us  [body(): pl.pallas_call(kernel, out_shape=shapes, in_specs=[hbm] * 6 + [vmem] * 8,...]
where the time goes in v3:
time: 164 us
  Pallas kernels  163 us (99%)
    pallas_call x1, Pallas kernels, body(): pl.pallas_call(kernel, out_shape=shapes, in_specs=[hbm] * 6 + [vmem] * 8,...  160 us

profile of v3, /device:TPU:1, one launch (start us, length us, event | category | flops | bytes accessed | tf_op | source)
XLA Modules:
  0.0 163.8 jit_solution(12380357208063125483)
XLA Ops:
  0.7 160.2 %encoder_layer.1 = (bf16[256,1024]{1,0:T(8,128)(2,1)}, f32[256,1024]{1,0:T(8,128)}, f32[3,16,512]{2,1,0:T(8,128)}, f32[16,512]{1,0:T(8,128)}, f32[16,2048]{1,0:T...) custom-call(bf16[256,1024]{1,0:T(8,128)(2,1)} %refs_0_.1, ...), custom_call_target="tpu_custom_call" | custom-call | flops 22000001024 | bytes 5000000 | tf_op jit(solution)/shard_map/encoder_layer/pallas_call | solution.py:861
  160.9 2.7 %hand_on.1 = (bf16[256,1024]{1,0:T(8,128)(2,1)}, f32[256,1024]{1,0:T(8,128)}, f32[3,16,512]{2,1,0:T(8,128)}, f32[16,512]{1,0:T(8,128)}, f32[16,2048]{1,0:T(8,128...) custom-call(bf16[256,1024]{1,0:T(8,128)(2,1)} %get-tuple-element.42., ...), custom_call_target="tpu_custom_call" | custom-call | tf_op jit(solution)/shard_map/hand_on/pallas_call | solution.py:904

commit v4 on v3

--- a/solution.py
+++ b/solution.py
@@ -17,8 +17,8 @@
 PIECES = (
     ((0, 0, 256), (1, 256, 256), (2, 512, 256)),
     ((1, 0, 128), (2, 128, 128)),
-    ((0, 0, 384), (1, 384, 384), (2, 768, 256)),
-    ((0, 0, 384), (1, 384, 256), (2, 640, 384)),
+    ((0, 0, 256), (1, 256, 384), (2, 640, 384)),
+    ((0, 0, 256), (1, 256, 384), (2, 640, 384)),
 )
 ORDER = (("x", "z", "y"), ("z", "y", "x"), ("y", "x", "z"))
 PIECE_LIST = [(g, i) for g in range(4) for i in range(len(PIECES[g]))]

time: 164 us -> 163 us (level)
  no operation moved by 1% of the time
where the time goes in v4:
time: 163 us
  Pallas kernels  162 us (99%)
    pallas_call x1, Pallas kernels, body(): pl.pallas_call(kernel, out_shape=shapes, in_specs=[hbm] * 6 + [vmem] * 8,...  159 us

profile of v4, /device:TPU:1, one launch (start us, length us, event | category | flops | bytes accessed | tf_op | source)
XLA Modules:
  0.0 162.9 jit_solution(5310175383450749828)
XLA Ops:
  0.7 159.4 %encoder_layer.1 = (bf16[256,1024]{1,0:T(8,128)(2,1)}, f32[256,1024]{1,0:T(8,128)}, f32[3,16,512]{2,1,0:T(8,128)}, f32[16,512]{1,0:T(8,128)}, f32[16,2048]{1,0:T...) custom-call(bf16[256,1024]{1,0:T(8,128)(2,1)} %refs_0_.1, ...), custom_call_target="tpu_custom_call" | custom-call | flops 22000001024 | bytes 5000000 | tf_op jit(solution)/shard_map/encoder_layer/pallas_call | solution.py:861
  160.0 2.7 %hand_on.1 = (bf16[256,1024]{1,0:T(8,128)(2,1)}, f32[256,1024]{1,0:T(8,128)}, f32[3,16,512]{2,1,0:T(8,128)}, f32[16,512]{1,0:T(8,128)}, f32[16,2048]{1,0:T(8,128...) custom-call(bf16[256,1024]{1,0:T(8,128)(2,1)} %get-tuple-element.42., ...), custom_call_target="tpu_custom_call" | custom-call | tf_op jit(solution)/shard_map/hand_on/pallas_call | solution.py:904
